TPU v7x, 512 devices: a whole 4x8x8 slice. The times are simulated.
512 devices in a mesh: section: 16 (over y_lo, x, core), tp: 32 (over z, y_hi).
Axes of the slice: x: 4, y: 8 (y_hi: 4, y_lo: 2; y = y_hi * 2 + y_lo), z: 8, core: 2. Of those that a mesh axis runs over, the one named last changes fastest.
Arguments:
- tokens: bfloat16 [512, 8192], P('tp', 'section'), may hold values from -24 to 24, as said below
- norm_gain: float32 [8192], P('section'), may hold values from 0.5 to 1.5
- gate_weight: bfloat16 [8192, 28672], P('section', 'tp'), may hold values from -0.0625 to 0.0625
- up_weight: bfloat16 [8192, 28672], P('section', 'tp'), may hold values from -0.0625 to 0.0625
- down_weight: bfloat16 [28672, 8192], P('tp', 'section'), may hold values from -0.03125 to 0.03125
- revisit: int32 [512], P('tp'), may hold values from 1 to 2, as said below
Outputs:
- revisited: bfloat16 [512, 8192], P('tp', 'section')
Inputs may be any that keep to these rules, and one draw needn't show every extreme that they name: tokens has rows and columns of different scales. Exactly 64 tokens have revisit 2; among the rows of one index of tp at most 8 do, and some index of tp has exactly 8.
All inputs are finite; a program needn't handle non-finite values.
Results may differ from a plain program's by a relative error of at most 0.017.
Values may be sent and summed in bfloat16 or wider, within the bound.
A program may use at most 64 MiB of HBM per device.

v0:
```python
import jax
import jax.numpy as jnp
from jax import lax
from jax.sharding import PartitionSpec as P


def normalize(values, norm_gain):
    squares = jnp.sum(values * values, axis=1)
    summed_sq = lax.psum(squares, "section")
    feature_count = values.shape[1] * lax.axis_size("section")
    scaling = lax.rsqrt(summed_sq / feature_count + 1e-05)
    return (values * scaling[:, None] * norm_gain[None, :]).astype(jnp.bfloat16)


def activate(gate_total, up_total):
    return (jax.nn.silu(gate_total) * up_total).astype(jnp.bfloat16)


def project(normed, gate_weight, up_weight, down_weight):
    gate_part = jnp.dot(normed, gate_weight, preferred_element_type=jnp.float32)
    up_part = jnp.dot(normed, up_weight, preferred_element_type=jnp.float32)
    gate_total, up_total = (
        lax.psum(gate_part.astype(jnp.bfloat16), "section").astype(jnp.float32),
        lax.psum(up_part.astype(jnp.bfloat16), "section").astype(jnp.float32),
    )
    hidden = activate(gate_total, up_total)
    return jnp.dot(hidden, down_weight, preferred_element_type=jnp.float32)


def body(tokens, norm_gain, gate_weight, up_weight, down_weight, revisit):
    tok_rows = tokens.shape[0]
    start_state = tokens.astype(jnp.float32)
    first_normed = normalize(start_state, norm_gain)
    gathered = lax.all_gather(first_normed, "tp", axis=0, tiled=True)
    down_part = project(gathered, gate_weight, up_weight, down_weight)
    delta_one = lax.psum_scatter(
        down_part.astype(jnp.bfloat16), "tp", scatter_dimension=0, tiled=True
    ).astype(jnp.float32)
    state_one = start_state + delta_one
    second_normed = normalize(state_one, norm_gain)
    active_rows = revisit == 2
    row_order = jnp.cumsum(active_rows.astype(jnp.int32)) - 1
    slot_total = tok_rows // 2
    slot_ids = jnp.arange(slot_total, dtype=jnp.int32)
    placing = (slot_ids[:, None] == row_order[None, :]) & active_rows[None, :]
    packed = jnp.dot(
        placing.astype(jnp.bfloat16), second_normed, preferred_element_type=jnp.float32
    ).astype(jnp.bfloat16)
    pooled = lax.all_gather(packed, "tp", axis=0, tiled=True)
    partial_value = project(pooled, gate_weight, up_weight, down_weight)
    returned = lax.psum_scatter(
        partial_value.astype(jnp.bfloat16), "tp", scatter_dimension=0, tiled=True
    ).astype(jnp.float32)
    placing_float = placing.astype(jnp.float32)
    revisit_delta = jnp.dot(placing_float.T, returned, precision=lax.Precision.HIGHEST)
    revisited = state_one + jnp.where(active_rows[:, None], revisit_delta, 0.0)
    return revisited.astype(jnp.bfloat16)


def solution(mesh):
    placed = (
        P("tp", "section"),
        P("section"),
        P("section", "tp"),
        P("section", "tp"),
        P("tp", "section"),
        P("tp"),
    )
    return jax.shard_map(
        body, mesh=mesh, in_specs=placed, out_specs=P("tp", "section"), check_vma=False
    )
```

profile of v0, /device:TPU:1, one launch (start us, length us, event | category | flops | bytes accessed | tf_op | source)
XLA Modules:
  0.0 950.6 jit_solution(8126399983588756826)
XLA Ops:
  6.5 0.9 fusion.15
  7.5 33.4 %psum.42 = f32[16]{0:T(128)S(1)} all-reduce(f32[16]{0:T(128)S(1)} %fusion.15), channel_id=1, replica_groups=mesh['section'=16,'tp'=32] {'section'}, use_global_device_ids=true, to_apply=%region_1.0 | all-reduce | flops 16 | bytes 128 | tf_op jit(solution)/shard_map/psum | solution.py:9
  40.8 0.8 fusion.17
  41.6 71.5 %all_gather.6 = bf16[512,512]{1,0:T(8,128)(2,1)S(1)} all-gather(bf16[16,512]{1,0:T(8,128)(2,1)S(1)} %fusion.17), channel_id=1, replica_groups=mesh['section'=16,'tp'=32] {'tp'}, dimensions={0}, use_global_device_ids=true | all-gather | bytes 540672 | tf_op jit(solution)/shard_map/all_gather | solution.py:34
  113.1 1.6 convolution_convert_fusion
  114.8 1.7 convolution_convert_fusion.1
  116.4 0.0 reduce-scatter.3.cloned.1.call-start
  116.5 137.6 %all-reduce.7.cloned.1.call-done = (bf16[512,896]{1,0:T(8,128)(2,1)}, bf16[512,896]{1,0:T(8,128)(2,1)}) async-done(((bf16[512,896]{1,0:T(8,128)(2,1)}, bf16[512,896]{1,0:T(8,128)(2,1)}), (bf16[512,896]{1,0:T(8,128)(2,1)}, bf16[512,896]{1,0:T(8,128)(2,1)})) %all-reduce.7.cloned.1.call-update) | async-done | bytes 1835024 | tf_op jit(solution)/shard_map/psum | solution.py:24
  254.2 3.1 convolution_convert_fusion.2
  257.3 0.0 all-reduce.5.cloned.1.call-start
  257.3 0.1 copy.8
  257.5 0.1 add_reduce_fusion
  257.6 222.8 %reduce-scatter.3.cloned.1.call-done = bf16[16,512]{1,0:T(8,128)(2,1)} async-done(((bf16[512,512]{1,0:T(8,128)(2,1)}), bf16[16,512]{1,0:T(8,128)(2,1)}) %reduce-scatter.3.cloned.1.call-update) | async-done | bytes 16400 | tf_op jit(solution)/shard_map/reduce_scatter | solution.py:36
  480.4 0.8 multiply_reduce_fusion
  481.2 31.6 %psum.45 = f32[16]{0:T(128)S(1)} all-reduce(f32[16]{0:T(128)S(1)} %multiply_reduce_fusion), channel_id=1, replica_groups=mesh['section'=16,'tp'=32] {'section'}, use_global_device_ids=true, to_apply=%region_7.8 | all-reduce | flops 16 | bytes 128 | tf_op jit(solution)/shard_map/psum | solution.py:9
  512.9 0.9 convolution_convert_fusion.6
  513.8 66.1 %all_gather.7 = bf16[256,512]{1,0:T(8,128)(2,1)S(1)} all-gather(bf16[8,512]{1,0:T(8,128)(2,1)S(1)} %convolution_convert_fusion.6), channel_id=1, replica_groups=mesh['section'=16,'tp'=32] {'tp'}, dimensions={0}, use_global_device_ids=true | all-gather | bytes 270336 | tf_op jit(solution)/shard_map/all_gather | solution.py:49
  579.9 1.2 convolution_convert_fusion.3
  581.1 1.3 convolution_convert_fusion.4
  582.4 0.0 reduce-scatter.5.cloned.1.call-start
  582.5 134.6 %all-reduce.5.cloned.1.call-done = (bf16[256,896]{1,0:T(8,128)(2,1)}, bf16[256,896]{1,0:T(8,128)(2,1)}) async-done(((bf16[256,896]{1,0:T(8,128)(2,1)}, bf16[256,896]{1,0:T(8,128)(2,1)}), (bf16[256,896]{1,0:T(8,128)(2,1)}, bf16[256,896]{1,0:T(8,128)(2,1)})) %all-reduce.5.cloned.1.call-update) | async-done | bytes 917520 | tf_op jit(solution)/shard_map/psum | solution.py:24
  717.0 2.4 convolution_convert_fusion.5
  719.4 223.1 %reduce-scatter.5.cloned.1.call-done = bf16[8,512]{1,0:T(8,128)(2,1)} async-done(((bf16[256,512]{1,0:T(8,128)(2,1)}), bf16[8,512]{1,0:T(8,128)(2,1)}) %reduce-scatter.5.cloned.1.call-update) | async-done | bytes 8208 | tf_op jit(solution)/shard_map/reduce_scatter | solution.py:51
  942.5 1.5 fusion.6
  (23 shorter events, 0.2 us)
Async XLA Ops:
  6.5 106.6 %copy-start = (bf16[512,896]{1,0:T(8,128)(2,1)S(1)}, bf16[512,896]{1,0:T(8,128)(2,1)}, u32[]{:S(2)}) copy-start(bf16[512,896]{1,0:T(8,128)(2,1)} %param.9) | copy-start | bytes 2752516
  6.5 247.6 %all-reduce.7.cloned.1.call-start = ((), (), s32[]{:S(2)}) async-start(), calls=%async_computation.5 | async-start | bytes 3670016 | tf_op jit(solution)/shard_map/psum | solution.py:24
  113.1 1.6 copy-start.1
  116.4 137.7 %copy-start.5 = (bf16[896,512]{1,0:T(8,128)(2,1)S(1)}, bf16[896,512]{1,0:T(8,128)(2,1)}, u32[]{:S(2)}) copy-start(bf16[896,512]{1,0:T(8,128)(2,1)} %param.10) | copy-start | bytes 2752516
  116.4 364.0 %reduce-scatter.3.cloned.1.call-start = ((), (), s32[]{:S(2)}) async-start(), calls=%async_computation.2 | async-start | bytes 540672 | tf_op jit(solution)/shard_map/reduce_scatter | solution.py:36
  254.1 3.2 copy-start.6
  254.1 226.3 %copy-start.2 = (bf16[16,512]{1,0:T(8,128)(2,1)S(1)}, bf16[16,512]{1,0:T(8,128)(2,1)}, u32[]{:S(2)}) copy-start(bf16[16,512]{1,0:T(8,128)(2,1)} %param.6) | copy-start | bytes 49156
  254.2 258.7 %copy-start.4 = (f32[512]{0:T(512)S(1)}, f32[512]{0:T(512)}, u32[]{:S(2)}) copy-start(f32[512]{0:T(512)} %param.7) | copy-start | bytes 6148
  257.3 459.8 %all-reduce.5.cloned.1.call-start = ((), (), s32[]{:S(2)}) async-start(), calls=%async_computation.4 | async-start | bytes 1835008 | tf_op jit(solution)/shard_map/psum | solution.py:24
  582.4 360.1 %reduce-scatter.5.cloned.1.call-start = ((), (), s32[]{:S(2)}) async-start(), calls=%async_computation.3 | async-start | bytes 270336 | tf_op jit(solution)/shard_map/reduce_scatter | solution.py:51
  717.0 225.5 %copy-start.3 = (bf16[16,512]{1,0:T(8,128)(2,1)S(1)}, bf16[16,512]{1,0:T(8,128)(2,1)}, u32[]{:S(2)}) copy-start(bf16[16,512]{1,0:T(8,128)(2,1)} %reduce-scatter.3.cloned.1.call-done) | copy-start | bytes 49156
Sparse Core Ops, SparseCore 0:
  116.6 137.5 all-reduce.6
  259.2 221.2 reduce-scatter.2
  582.5 134.4 all-reduce.4
  721.9 220.5 reduce-scatter.4
where the time goes:
time: 955 us; the launch traced here: 951 us
  waiting for transfers between devices  718 us (75%)
  blocking collectives  203 us (21%)
  matrix products  13.6 us (1%)
  between operations  13.2 us (1%)
    psum x2, waiting for transfers between devices, project(): lax.psum(up_part.astype(jnp.bfloat16), 'section').astype(jnp.float32)  272 us
    reduce_scatter x1, waiting for transfers between devices, body(): lax.psum_scatter(partial_value.astype(jnp.bfloat16), 'tp', scatter_dimens...  223 us
    reduce_scatter x1, waiting for transfers between devices, body(): lax.psum_scatter(down_part.astype(jnp.bfloat16), 'tp', scatter_dimension=...  223 us
    all_gather x1, blocking collectives, body(): gathered = lax.all_gather(first_normed, 'tp', axis=0, tiled=True)  71.5 us
    all_gather x1, blocking collectives, body(): pooled = lax.all_gather(packed, 'tp', axis=0, tiled=True)  66.1 us
    psum x2, blocking collectives, normalize(): summed_sq = lax.psum(squares, 'section')  65 us
  transfers between devices with their start and end apart: 4, of which 4 were waited for; matrix products, arithmetic and copies ran while one was open for 0% of the time, Pallas kernels for 0%

commit v1 on v0

v1 whole, which is shorter than its diff:
```python
import functools
import jax
import jax.numpy as jnp
from jax import lax
from jax.experimental import pallas as pl
from jax.experimental.pallas import tpu as pltpu
from jax.sharding import PartitionSpec as P

BF, F32 = jnp.bfloat16, jnp.float32
GROUPS = ((0, 256), (256, 256), (512, 256), (768, 128))
FEATURES = 8192.0
EPS = 1e-5
LAST = 99


def mo(value, unit):
    return pl.multiple_of(value, unit)


def eye(rows, lanes, offset=0):
    row = lax.broadcasted_iota(jnp.int32, (rows, lanes), 0)
    lane = lax.broadcasted_iota(jnp.int32, (rows, lanes), 1)
    return lane == row + offset


class Wire:
    def __init__(self, send_sem, recv_sem):
        self.send_sem, self.recv_sem = send_sem, recv_sem
        self.count, self.sent = 0, []

    def slot(self):
        self.count += 1
        return self.count - 1

    def send(self, src, dst, slot, dev):
        copy = pltpu.make_async_remote_copy(
            src_ref=src, dst_ref=dst, send_sem=self.send_sem.at[slot], recv_sem=self.recv_sem.at[slot],
            device_id=dev, device_id_type=pl.DeviceIdType.MESH)
        copy.start()
        self.sent.append(copy)

    def recv(self, dst, slot, dev):
        pltpu.make_async_remote_copy(
            src_ref=dst, dst_ref=dst, send_sem=self.send_sem.at[slot], recv_sem=self.recv_sem.at[slot],
            device_id=dev, device_id_type=pl.DeviceIdType.MESH).wait_recv()

    def drain(self):
        for copy in self.sent:
            copy.wait_send()


def kernel(upto, tok, gain, rev_row, rev_col, wg, wu, wd, out,
           X, XG, W, WD, F, snd, own, crecv, fwdp, fwdm, dirp, dirm, ysnd, yrecv, tot, H,
           D, upb, dnb, tsum, tbf, yb, SS, SSr, S2, S2r,
           X2, C, G2, c2r, x2r, y2s, y2r, t2, H2, D2, upb2, dnb2, tsum2, tbf2, yb2, st,
           wsem, send_sem, recv_sem):
    s, t = lax.axis_index("section"), lax.axis_index("tp")
    c, x, yl = s % 2, (s // 2) % 4, s // 8
    z, yh = t // 4, t % 4
    wire = Wire(send_sem, recv_sem)

    def sec(dc=0, dx=0, dy=0):
        return ((((yl + dy) % 2) * 4 + (x + dx) % 4) * 2 + (c + dc) % 2, t)

    def tpd(dz=0, dh=0):
        return (s, ((z + dz + 8) % 8) * 4 + (yh + dh) % 4)

    core, ydev = sec(dc=1), sec(dy=1)
    xs = {j: sec(dx=j) for j in (1, 2, 3)}
    ups, downs = tpd(dz=1), tpd(dz=-1)
    yhs = {j: tpd(dh=j) for j in (1, 2, 3)}

    barrier = pltpu.get_barrier_semaphore()
    peers = [core, ydev, ups, downs] + list(xs.values()) + list(yhs.values())
    for peer in peers:
        pl.semaphore_signal(barrier, inc=1, device_id=peer, device_id_type=pl.DeviceIdType.MESH)

    loads = []
    for g, (lo, w) in enumerate(GROUPS):
        loads.append(pltpu.make_async_copy(wg.at[:, lo:lo + w], W.at[:, 2 * lo:2 * lo + w], wsem.at[2 * g]))
        loads.append(pltpu.make_async_copy(wu.at[:, lo:lo + w], W.at[:, 2 * lo + w:2 * lo + 2 * w], wsem.at[2 * g + 1]))
    load_down = pltpu.make_async_copy(wd, WD, wsem.at[8])
    for load in loads:
        load.start()
    load_down.start()
    X[pl.ds(mo(t * 16, 16), 16), :] = tok[...]
    flag_row = jnp.where(rev_row[...] == 2, 1.0, 0.0)
    F[t] = jnp.concatenate([flag_row, jnp.zeros((1, 112), F32)], axis=1)
    pl.semaphore_wait(barrier, len(peers))

    def finish():
        wire.drain()

    def ring_gather(buf, flags):
        def rows(zz, j):
            return buf.at[pl.ds(mo(((((zz + 16) % 8) * 4) + (yh - j + 4) % 4) * 16, 16), 16), :]

        def frow(zz):
            return flags.at[pl.ds(((zz + 16) % 8) * 4, 4)]

        yslot = {j: wire.slot() for j in (1, 2, 3)}
        uslot = {(k, j): wire.slot() for k in range(4) for j in range(4)}
        dslot = {(k, j): wire.slot() for k in range(4) for j in range(4)}
        order = (0, 1, 3, 2)
        mine = rows(z, 0)
        wire.send(mine, mine, uslot[0, 0], ups)
        wire.send(mine, mine, dslot[0, 0], downs)
        for j in (1, 3, 2):
            wire.send(mine, mine, yslot[j], yhs[j])
        if flags is not None:
            fy = {j: wire.slot() for j in (1, 2, 3)}
            for j in (1, 2, 3):
                wire.send(flags.at[pl.ds(t, 1)], flags.at[pl.ds(t, 1)], fy[j], yhs[j])
        for k in range(4):
            for j in order:
                if k == 0:
                    if j == 0:
                        continue
                    wire.recv(rows(z, j), yslot[j], yhs[j])
                    wire.send(rows(z, j), rows(z, j), uslot[k, j], ups)
                    wire.send(rows(z, j), rows(z, j), dslot[k, j], downs)
                    continue
                wire.recv(rows(z - k, j), uslot[k - 1, j], downs)
                if k < 3 or j in (0, 1):
                    wire.send(rows(z - k, j), rows(z - k, j), uslot[k, j], ups)
                wire.recv(rows(z + k, j), dslot[k - 1, j], ups)
                if k < 3 or j in (2, 3):
                    wire.send(rows(z + k, j), rows(z + k, j), dslot[k, j], downs)
        for j in (0, 1):
            wire.recv(rows(z - 4, j), uslot[3, j], downs)
        for j in (3, 2):
            wire.recv(rows(z + 4, j), dslot[3, j], ups)
        if flags is None:
            return None

        def step(k):
            if k == 0:
                for j in (1, 2, 3):
                    wire.recv(flags.at[pl.ds(z * 4 + (yh - j + 4) % 4, 1)], fy[j], yhs[j])
            else:
                wire.recv(frow(z - k), step.up[k - 1], downs)
                if k < 4:
                    wire.recv(frow(z + k), step.down[k - 1], ups)
            if k < 4:
                step.up[k] = wire.slot()
                wire.send(frow(z - k), frow(z - k), step.up[k], ups)
            if k < 3:
                step.down[k] = wire.slot()
                wire.send(frow(z + k), frow(z + k), step.down[k], downs)
        step.up, step.down = {}, {}
        return step

    def ring_reduce(src, ub, db, ts, tb, ybuf, block_done):
        def part(off, h):
            return src.at[pl.ds(mo(((z + off + 8) % 8) * 64 + h * 32, 32), 32), :]

        us = {(k, h): wire.slot() for k in range(4) for h in range(2)}
        ds = {(k, h): wire.slot() for k in range(4) for h in range(2)}
        block_done(4)
        wire.send(part(4, 0), ub.at[0, 0:32, :], us[0, 0], ups)
        wire.send(part(4, 1), db.at[0, 32:64, :], ds[0, 1], downs)
        for k in (1, 2, 3):
            block_done(4 - k)
            for h in ((1, 0) if k == 1 else (0, 1)):
                hu, hd = h, 1 - h
                if k > 1 or hu == 0:
                    got = ub.at[k - 1, hu * 32:hu * 32 + 32, :]
                    wire.recv(got, us[k - 1, hu], downs)
                    mine = part(4 - k, hu)
                    mine[...] = (mine[...].astype(F32) + got[...].astype(F32)).astype(BF)
                wire.send(part(4 - k, hu), ub.at[k, hu * 32:hu * 32 + 32, :], us[k, hu], ups)
                if k > 1 or hd == 1:
                    got = db.at[k - 1, hd * 32:hd * 32 + 32, :]
                    wire.recv(got, ds[k - 1, hd], ups)
                    mine = part(k - 4, hd)
                    mine[...] = (mine[...].astype(F32) + got[...].astype(F32)).astype(BF)
                wire.send(part(k - 4, hd), db.at[k, hd * 32:hd * 32 + 32, :], ds[k, hd], downs)
        for h in (0, 1):
            a, b = ub.at[3, h * 32:h * 32 + 32, :], db.at[3, h * 32:h * 32 + 32, :]
            wire.recv(a, us[3, h], downs)
            wire.recv(b, ds[3, h], ups)
            total = part(0, h)[...].astype(F32) + a[...].astype(F32) + b[...].astype(F32)
            ts[h * 32:h * 32 + 32, :] = total
            tb[h * 32:h * 32 + 32, :] = total.astype(BF)
        ys = {j: wire.slot() for j in (1, 2, 3)}
        for j in (2, 1, 3):
            wire.send(tb.at[pl.ds(mo(((yh + j) % 4) * 16, 16), 16), :], ybuf.at[j - 1], ys[j], yhs[j])
        total = ts[pl.ds(mo(yh * 16, 16), 16), :]
        for j in (1, 3, 2):
            wire.recv(ybuf.at[j - 1], ys[j], yhs[j])
            total = total + ybuf[j - 1].astype(F32)
        return total

    fstep = ring_gather(X, F)
    if upto < 1:
        for k in range(5):
            fstep(k)
        out[...] = X[pl.ds(mo(t * 16, 16), 16), :]
        return finish()

    g = gain[...]
    for b in range(4):
        part_cols = []
        for q in range(4):
            lo = b * 128 + q * 32
            v = X[lo:lo + 32, :].astype(F32)
            XG[lo:lo + 32, :] = (v * g).astype(BF)
            part_cols.append(jnp.sum(v * v, axis=1, keepdims=True))
        col = jnp.concatenate(part_cols, axis=0)
        SS[b:b + 1, :] = jnp.sum(jnp.where(eye(128, 128), col, 0.0), axis=0, keepdims=True)
    SS[4:8, :] = jnp.zeros((4, 128), F32)

    def sq_rounds(ss, rr):
        slots = [wire.slot() for _ in range(5)]

        def start(n):
            if n == 0:
                wire.send(ss, rr.at[0], slots[0], core)
            if n == 1:
                wire.recv(rr.at[0], slots[0], core)
                ss2 = rr.at[5]
                ss2[...] = ss[...] + rr[0]
                for j in (1, 2, 3):
                    wire.send(ss2, rr.at[j], slots[j], xs[j])
            if n == 2:
                for j in (1, 2, 3):
                    wire.recv(rr.at[j], slots[j], xs[j])
                ss3 = rr.at[6]
                ss3[...] = rr[5] + rr[1] + rr[2] + rr[3]
                wire.send(ss3, rr.at[4], slots[4], ydev)
            if n == 3:
                wire.recv(rr.at[4], slots[4], ydev)
                rr[7] = rr[6] + rr[4]
        return start

    sq = sq_rounds(SS, SSr)
    sq(0)

    def gate_up(row0, g_index, dst):
        lo, w = GROUPS[g_index]

        @pl.loop(0, 2)
        def _(i):
            r = mo(i * 128, 128)
            dst[pl.ds(r, 128), 2 * lo:2 * lo + 2 * w] = jnp.dot(
                XG[pl.ds(mo(row0 + r, 128), 128), :], W[:, 2 * lo:2 * lo + 2 * w],
                preferred_element_type=F32).astype(BF)

    def cols(g_index):
        lo, w = GROUPS[g_index]
        return slice(2 * lo, 2 * lo + 2 * w)

    NG = len(GROUPS)
    cslot = [wire.slot() for _ in range(NG)]
    for p in range(NG):
        loads[2 * p].wait()
        loads[2 * p + 1].wait()
        gate_up((1 - c) * 256, p, snd)
        wire.send(snd.at[:, cols(p)], crecv.at[:, cols(p)], cslot[p], core)
    for k in range(5):
        fstep(k)

    def blk(off, h):
        return pl.ds(mo(((x + off) % 4) * 64 + h * 32, 32), 32)

    xslot = [[wire.slot() for _ in range(6)] for _ in range(NG)]
    for p in range(NG):
        gate_up(c * 256, p, own)
        wire.recv(crecv.at[:, cols(p)], cslot[p], core)

        @pl.loop(0, 8)
        def _(i):
            r = pl.ds(mo(i * 32, 32), 32)
            own[r, cols(p)] = (own[r, cols(p)].astype(F32) + crecv[r, cols(p)].astype(F32)).astype(BF)
        wire.send(own.at[blk(2, 0), cols(p)], fwdp.at[:, cols(p)], xslot[p][0], xs[1])
        wire.send(own.at[blk(2, 1), cols(p)], fwdm.at[:, cols(p)], xslot[p][1], xs[3])
        wire.send(own.at[blk(1, 1), cols(p)], dirp.at[32:64, cols(p)], xslot[p][2], xs[1])
        wire.send(own.at[blk(3, 0), cols(p)], dirm.at[0:32, cols(p)], xslot[p][3], xs[3])
        if p == 0:
            sq(1)
    if upto < 2:
        for p in range(NG):
            wire.recv(fwdp.at[:, cols(p)], xslot[p][0], xs[3])
            wire.recv(fwdm.at[:, cols(p)], xslot[p][1], xs[1])
            wire.recv(dirp.at[32:64, cols(p)], xslot[p][2], xs[3])
            wire.recv(dirm.at[0:32, cols(p)], xslot[p][3], xs[1])
        sq(2)
        sq(3)
        load_down.wait()
        out[...] = own[0:16, 0:512] + fwdp[0:16, 0:512]
        return finish()
    for p in range(NG):
        wire.recv(fwdp.at[:, cols(p)], xslot[p][0], xs[3])
        r = blk(1, 0)
        own[r, cols(p)] = (own[r, cols(p)].astype(F32) + fwdp[:, cols(p)].astype(F32)).astype(BF)
        wire.send(own.at[r, cols(p)], dirp.at[0:32, cols(p)], xslot[p][4], xs[1])
        wire.recv(fwdm.at[:, cols(p)], xslot[p][1], xs[1])
        r = blk(3, 1)
        own[r, cols(p)] = (own[r, cols(p)].astype(F32) + fwdm[:, cols(p)].astype(F32)).astype(BF)
        wire.send(own.at[r, cols(p)], dirm.at[32:64, cols(p)], xslot[p][5], xs[3])
    sq(2)
    yslot = [wire.slot() for _ in range(NG)]
    mine, other = yl, 1 - yl
    for p in range(NG):
        wire.recv(dirp.at[32:64, cols(p)], xslot[p][2], xs[3])
        wire.recv(dirm.at[0:32, cols(p)], xslot[p][3], xs[1])
        wire.recv(dirp.at[0:32, cols(p)], xslot[p][4], xs[3])
        wire.recv(dirm.at[32:64, cols(p)], xslot[p][5], xs[1])

        def xsum(h):
            hr = pl.ds(mo(h * 32, 32), 32)
            return (own[blk(0, h), cols(p)].astype(F32) + dirp[hr, cols(p)].astype(F32)
                    + dirm[hr, cols(p)].astype(F32))
        ysnd[:, cols(p)] = xsum(other).astype(BF)
        wire.send(ysnd.at[:, cols(p)], yrecv.at[:, cols(p)], yslot[p], ydev)
        tot[:, cols(p)] = xsum(mine)
    sq(3)
    row0 = c * 256 + x * 64 + yl * 32

    def scale_of(rr, first, count):
        line = rr[7, pl.ds(first // 128, 1), :]
        picked = jnp.where(eye(count, 128, first % 128), line, 0.0)
        return lax.rsqrt(jnp.sum(picked, axis=1, keepdims=True) / FEATURES + EPS)

    scale = scale_of(SSr, row0, 32)

    def act(gate, up):
        return (gate / (1.0 + jnp.exp(-gate)) * up).astype(BF)

    def hrows(off, h):
        return pl.ds(mo(c * 256 + ((x + off) % 4) * 64 + h * 32, 32), 32)

    hy = [wire.slot() for _ in range(NG)]
    hx = [[wire.slot() for _ in range(6)] for _ in range(NG)]
    hc = [wire.slot() for _ in range(NG)]

    def hcols(p):
        lo, w = GROUPS[p]
        return slice(lo, lo + w)

    def hsend(off, h, p, slot, dev):
        ref = H.at[hrows(off, h), hcols(p)]
        wire.send(ref, ref, slot, dev)

    def hrecv(off, h, p, slot, dev):
        wire.recv(H.at[hrows(off, h), hcols(p)], slot, dev)

    for p in range(NG):
        lo, w = GROUPS[p]
        wire.recv(yrecv.at[:, cols(p)], yslot[p], ydev)
        gate = (tot[:, 2 * lo:2 * lo + w] + yrecv[:, 2 * lo:2 * lo + w].astype(F32)) * scale
        up = (tot[:, 2 * lo + w:2 * lo + 2 * w] + yrecv[:, 2 * lo + w:2 * lo + 2 * w].astype(F32)) * scale
        H[hrows(0, mine), hcols(p)] = act(gate, up)
        hsend(0, mine, p, hy[p], ydev)
        hsend(0, mine, p, hx[p][0], xs[1])
        hsend(0, mine, p, hx[p][1], xs[3])
    if upto < 3:
        for p in range(NG):
            hrecv(0, other, p, hy[p], ydev)
            hrecv(3, mine, p, hx[p][0], xs[3])
            hrecv(1, mine, p, hx[p][1], xs[1])
        load_down.wait()
        out[...] = H[0:16, 0:512]
        return finish()
    for p in range(NG):
        hrecv(0, other, p, hy[p], ydev)
        hsend(0, other, p, hx[p][2], xs[1])
        hsend(0, other, p, hx[p][3], xs[3])
        hrecv(3, mine, p, hx[p][0], xs[3])
        hsend(3, mine, p, hx[p][4], xs[1])
        hrecv(1, mine, p, hx[p][1], xs[1])
    for p in range(NG):
        hrecv(3, other, p, hx[p][2], xs[3])
        hrecv(1, other, p, hx[p][3], xs[1])
        hsend(1, other, p, hx[p][5], xs[3])
    for p in range(NG):
        hrecv(2, mine, p, hx[p][4], xs[3])
        hrecv(2, other, p, hx[p][5], xs[1])
        half = H.at[pl.ds(mo(c * 256, 256), 256), hcols(p)]
        wire.send(half, half, hc[p], core)
    for p in range(NG):
        wire.recv(H.at[pl.ds(mo((1 - c) * 256, 256), 256), hcols(p)], hc[p], core)
    load_down.wait()
    if upto < 4:
        out[...] = H[0:16, 0:512]
        return finish()

    def down_pair(off):
        a = pl.ds(mo(((z + off) % 8) * 64, 64), 64)
        b = pl.ds(mo(((z - off + 8) % 8) * 64, 64), 64)
        if off == 4:
            b = pl.ds(mo(z * 64, 64), 64)
        rows = jnp.concatenate([H[a, :], H[b, :]], axis=0)
        prod = jnp.dot(rows, WD[...], preferred_element_type=F32).astype(BF)
        D[a, :] = prod[0:64]
        D[b, :] = prod[64:128]

    delta = ring_reduce(D, upb, dnb, tsum, tbf, yb, down_pair)
    state = tok[...].astype(F32) + delta
    st[...] = state
    if upto < 5:
        out[...] = state.astype(BF)
        return finish()

    active_row = rev_row[...] == 2
    active_col = rev_col[...] == 2
    sub = lax.broadcasted_iota(jnp.int32, (16, 16), 0)
    lane = lax.broadcasted_iota(jnp.int32, (16, 16), 1)
    place_row = jnp.sum(jnp.where((sub <= lane) & active_col, 1, 0), axis=0, keepdims=True) - 1
    place_col = jnp.sum(jnp.where((lane <= sub) & active_row, 1, 0), axis=1, keepdims=True) - 1
    picks = jnp.where((sub % 8 == place_row) & active_row, 1.0, 0.0).astype(BF)
    picked = jnp.dot(picks, (state * g).astype(BF), preferred_element_type=F32)
    fold = lax.broadcasted_iota(jnp.int32, (16, 256), 0) < 8
    X2[pl.ds(mo(t * 16, 16), 16), :] = jnp.where(fold, picked[:, 0:256], picked[:, 256:512]).astype(BF)
    ring_gather(X2, None)
    if upto < 6:
        out[...] = X2[0:16, :][:, 0:1].astype(F32).astype(BF) + state.astype(BF)
        return finish()

    counts = jnp.sum(F[...].reshape(32, 128), axis=1, keepdims=True)
    owner = lax.broadcasted_iota(jnp.int32, (32, 512), 1) // 16
    unit = lax.broadcasted_iota(jnp.int32, (32, 512), 0)
    before = jnp.sum(jnp.where(unit < owner, counts, 0.0), axis=0, keepdims=True)
    here = jnp.sum(jnp.where(unit == owner, counts, 0.0), axis=0, keepdims=True)
    slot_lane = lax.broadcasted_iota(jnp.int32, (1, 512), 1) % 16
    place = (slot_lane % 8).astype(F32)
    goal = jnp.where(place < here, before + place, -1.0)
    want = lax.broadcasted_iota(jnp.int32, (64, 512), 0).astype(F32)
    hit = jnp.where(goal == want, 1.0, 0.0)
    left = jnp.where(slot_lane < 8, hit, 0.0).astype(BF)
    right = jnp.where(slot_lane >= 8, hit, 0.0).astype(BF)
    C[:, 0:256] = jnp.dot(left, X2[...], preferred_element_type=F32).astype(BF)
    C[:, 256:512] = jnp.dot(right, X2[...], preferred_element_type=F32).astype(BF)
    unscaled = C[...].astype(F32) / g
    col = jnp.sum(unscaled * unscaled, axis=1, keepdims=True)
    S2[...] = jnp.zeros((8, 128), F32)
    S2[0:1, :] = jnp.sum(jnp.where(eye(64, 128), col, 0.0), axis=0, keepdims=True)
    sq2 = sq_rounds(S2, S2r)
    sq2(0)
    for p in range(NG):
        lo, w = GROUPS[p]
        prod = jnp.dot(C[...], W[:, cols(p)], preferred_element_type=F32).astype(BF)
        G2[:, 512 * p:512 * p + w] = prod[:, 0:w]
        G2[:, 512 * p + 256:512 * p + 256 + w] = prod[:, w:2 * w]
        if w < 256:
            G2[:, 512 * p + w:512 * p + 256] = jnp.zeros((64, 256 - w), BF)
            G2[:, 512 * p + 256 + w:512 * p + 512] = jnp.zeros((64, 256 - w), BF)
    slot = wire.slot()
    wire.send(G2.at[pl.ds(mo((1 - c) * 32, 32), 32), :], c2r, slot, core)
    mine_rows = pl.ds(mo(c * 32, 32), 32)
    wire.recv(c2r, slot, core)
    G2[mine_rows, :] = (G2[mine_rows, :].astype(F32) + c2r[...].astype(F32)).astype(BF)
    slots = {j: wire.slot() for j in (1, 2, 3)}
    for j in (2, 1, 3):
        wire.send(G2.at[mine_rows, pl.ds(mo(((x + j) % 4) * 512, 512), 512)], x2r.at[j - 1], slots[j], xs[j])
    sq2(1)
    for j in (1, 2, 3):
        wire.recv(x2r.at[j - 1], slots[j], xs[j])
    sum2 = G2[mine_rows, pl.ds(mo(x * 512, 512), 512)].astype(F32)
    for j in (1, 2, 3):
        sum2 = sum2 + x2r[j - 1].astype(F32)
    t2[...] = sum2
    y2s[...] = sum2.astype(BF)
    slot = wire.slot()
    wire.send(y2s.at[pl.ds(mo(other * 16, 16), 16), :], y2r, slot, ydev)
    sq2(2)
    sq2(3)
    scale2 = scale_of(S2r, c * 32 + yl * 16, 16)
    wire.recv(y2r, slot, ydev)
    full = (t2[pl.ds(mo(mine * 16, 16), 16), :] + y2r[...].astype(F32)) * scale2

    def h2(yy, xx):
        return H2.at[pl.ds(mo(c * 32 + yy * 16, 16), 16), pl.ds(mo(xx * 256, 256), 256)]

    h2(mine, x)[...] = act(full[:, 0:256], full[:, 256:512])
    slot = wire.slot()
    wire.send(h2(mine, x), h2(mine, x), slot, ydev)
    slots = {(j, h): wire.slot() for j in (1, 2, 3) for h in (0, 1)}
    for j in (2, 1, 3):
        wire.send(h2(mine, x), h2(mine, x), slots[j, 0], xs[j])
    wire.recv(h2(other, x), slot, ydev)
    for j in (2, 1, 3):
        wire.send(h2(other, x), h2(other, x), slots[j, 1], xs[j])
    for j in (1, 2, 3):
        wire.recv(h2(mine, (x + 4 - j) % 4), slots[j, 0], xs[j])
        wire.recv(h2(other, (x + 4 - j) % 4), slots[j, 1], xs[j])
    slot = wire.slot()
    wire.send(H2.at[mine_rows, :], H2.at[mine_rows, :], slot, core)
    wire.recv(H2.at[pl.ds(mo((1 - c) * 32, 32), 32), :], slot, core)
    if upto < 7:
        out[...] = H2[0:16, 0:512]
        return finish()
    down2 = jnp.dot(H2[:, 0:896], WD[...], preferred_element_type=F32).astype(BF)
    spread = (((0,), (0,)), ((), ()))
    D2[...] = (lax.dot_general(left, down2[:, 0:256], spread, preferred_element_type=F32)
               + lax.dot_general(right, down2[:, 256:512], spread, preferred_element_type=F32)).astype(BF)
    back = ring_reduce(D2, upb2, dnb2, tsum2, tbf2, yb2, lambda off: None)
    acc_l = jnp.zeros((16, 256), F32)
    acc_r = jnp.zeros((16, 256), F32)
    for k in range(8):
        put = jnp.where((place_col == k) & active_col, 1.0, 0.0)
        acc_l = acc_l + put * back[k:k + 1, :]
        acc_r = acc_r + put * back[k + 8:k + 9, :]
    out[...] = (st[...] + jnp.concatenate([acc_l, acc_r], axis=1)).astype(BF)
    finish()


def body(upto, tokens, norm_gain, gate_weight, up_weight, down_weight, revisit):
    vm = lambda *shape: pltpu.VMEM(shape, BF)
    vf = lambda *shape: pltpu.VMEM(shape, F32)
    vspec, anyspec = pl.BlockSpec(memory_space=pltpu.VMEM), pl.BlockSpec(memory_space=pl.ANY)
    scratch = [
        vm(512, 512), vm(512, 512), vm(512, 1792), vm(896, 512), vf(32, 1, 128),
        vm(256, 1792), vm(256, 1792), vm(256, 1792), vm(32, 1792), vm(32, 1792), vm(64, 1792), vm(64, 1792),
        vm(32, 1792), vm(32, 1792), vf(32, 1792), vm(512, 896),
        vm(512, 512), vm(4, 64, 512), vm(4, 64, 512), vf(64, 512), vm(64, 512), vm(3, 16, 512),
        vf(8, 128), vf(8, 8, 128), vf(8, 128), vf(8, 8, 128),
        vm(512, 256), vm(64, 512), vm(64, 2048), vm(32, 2048), vm(3, 32, 512), vm(32, 512), vm(16, 512), vf(32, 512),
        vm(64, 1024), vm(512, 256), vm(4, 64, 256), vm(4, 64, 256), vf(64, 256), vm(64, 256), vm(3, 16, 256),
        vf(16, 512),
        pltpu.SemaphoreType.DMA((9,)), pltpu.SemaphoreType.DMA((260,)), pltpu.SemaphoreType.DMA((260,)),
    ]
    return pl.pallas_call(
        functools.partial(kernel, upto),
        out_shape=jax.ShapeDtypeStruct((16, 512), BF),
        in_specs=[vspec] * 4 + [anyspec] * 3,
        out_specs=vspec,
        scratch_shapes=scratch,
        compiler_params=pltpu.CompilerParams(
            collective_id=0, has_side_effects=True, vmem_limit_bytes=40 * 1024 * 1024),
        cost_estimate=pl.CostEstimate(flops=2000000000, bytes_accessed=3000000, transcendentals=30000),
        name="two_pass_block",
    )(tokens, norm_gain.reshape(1, 512), revisit.reshape(1, 16), revisit.reshape(16, 1),
      gate_weight, up_weight, down_weight)


def solution(mesh, upto=LAST):
    placed = (P("tp", "section"), P("section"), P("section", "tp"), P("section", "tp"), P("tp", "section"), P("tp"))
    return jax.shard_map(functools.partial(body, upto), mesh=mesh, in_specs=placed,
                         out_specs=P("tp", "section"), check_vma=False)
```

time: 955 us -> 148 us (0.15)
  waiting for transfers between devices: 718 us -> 0 us
  blocking collectives: 203 us -> 0 us
  Pallas kernels: 0 us -> 139 us
  matrix products: 13.6 us -> 0 us
  between operations: 13.2 us -> 0.02 us
    reduce_scatter x2 -> x0, waiting for transfers between devices: 446 us -> none  [the longest x1 223 us: body(): lax.psum_scatter(partial_value.astype(jnp.bfloat16), 'tp', scatter_dimens...]
    psum x2 -> x0, waiting for transfers between devices: 272 us -> none  [project(): lax.psum(up_part.astype(jnp.bfloat16), 'section').astype(jnp.float32)]
    pallas_call x0 -> x1, Pallas kernels: none -> 139 us  [body(): pl.pallas_call(functools.partial(kernel, upto), out_shape=jax.ShapeDtypeS...]
    all_gather x2 -> x0, blocking collectives: 138 us -> none  [the longest x1 71.5 us: body(): gathered = lax.all_gather(first_normed, 'tp', axis=0, tiled=True)]
    psum x2 -> x0, blocking collectives: 65 us -> none  [normalize(): summed_sq = lax.psum(squares, 'section')]
    dot_general x8 -> x0, matrix products: 13.6 us -> none  [the longest x2 5.45 us: project(): return jnp.dot(hidden, down_weight, preferred_element_type=jnp.float32)]
  transfers between devices with their start and end apart: 4 -> 0, of which waited for: 4 -> 0; matrix products, arithmetic and copies ran while one was open for 0% -> 0% of each run, Pallas kernels for 0% -> 0%
where the time goes in v1:
time: 148 us; the launch traced here: 145 us
  Pallas kernels  139 us (94%)
  local copies, waits for them, and re-layouts  6.2 us (4%)
    pallas_call x1, Pallas kernels, body(): pl.pallas_call(functools.partial(kernel, upto), out_shape=jax.ShapeDtypeS...  139 us
    unnamed x13, local copies, waits for them, and re-layouts  6.11 us

profile of v1, /device:TPU:1, one launch (start us, length us, event | category | flops | bytes accessed | tf_op | source)
XLA Modules:
  0.0 145.5 jit_solution(9572775735776420929)
XLA Ops:
  0.0 0.0 copy-start
  0.0 0.7 copy-done
  0.7 0.0 copy-start.5
  0.7 0.1 copy.7.rev_col
  0.7 0.6 copy-done.5
  1.3 0.0 copy-start.1
  1.3 1.2 copy-done.1
  2.5 0.0 copy-start.2
  2.5 1.2 copy-done.2
  3.7 0.0 copy-start.3
  3.7 1.2 copy-done.3
  4.9 0.0 copy-start.4
  4.9 0.7 copy-done.4
  5.6 139.2 %two_pass_block.1 = bf16[16,512]{1,0:T(8,128)(2,1)S(1)} custom-call(bf16[16,512]{1,0:T(8,128)(2,1)S(1)} %copy-done.4, f32[1,512]{1,0:T(1,128)S(1)} %bitcast.5, s32[1,16]{1,0:T(1,128)S(1)} %bitcast.4, s32[16,1]{1,0:T(8,128)S(1)} %copy.7.rev_col, bf16[512,896]{1,0:T(8,128)(2,1)S(1)} %copy-done.1, bf16[512,896]{1,0:T(8,128)(2,1)S(1)} %copy-done.2, ...), custom_call_target="tpu_custom_call" | custom-call | flops 2000000000 | bytes 3000000 | tf_op jit(solution)/shard_map/two_pass_block/pallas_call | solution.py:523
  144.9 0.6 copy.9
Async XLA Ops:
  0.0 0.7 copy-start
  0.7 0.7 copy-start.5
  1.3 1.2 copy-start.1
  2.5 1.2 copy-start.2
  3.7 1.2 copy-start.3
  4.9 0.7 copy-start.4

commit v2 on v0

v2 whole, which is shorter than its diff:
```python
import functools
import jax
import jax.numpy as jnp
from jax import lax
from jax.experimental import pallas as pl
from jax.experimental.pallas import tpu as pltpu
from jax.sharding import PartitionSpec as P

BF, F32 = jnp.bfloat16, jnp.float32
GROUPS = ((0, 256), (256, 256), (512, 256), (768, 128))
FEATURES = 8192.0
EPS = 1e-5
LAST = 99


def mo(value, unit):
    return pl.multiple_of(value, unit)


def eye(rows, lanes, offset=0):
    row = lax.broadcasted_iota(jnp.int32, (rows, lanes), 0)
    lane = lax.broadcasted_iota(jnp.int32, (rows, lanes), 1)
    return lane == row + offset


class Wire:
    def __init__(self, send_sem, recv_sem):
        self.send_sem, self.recv_sem = send_sem, recv_sem
        self.count, self.sent = 0, []

    def slot(self):
        self.count += 1
        return self.count - 1

    def send(self, src, dst, slot, dev):
        copy = pltpu.make_async_remote_copy(
            src_ref=src, dst_ref=dst, send_sem=self.send_sem.at[slot], recv_sem=self.recv_sem.at[slot],
            device_id=dev, device_id_type=pl.DeviceIdType.MESH)
        copy.start()
        self.sent.append(copy)

    def recv(self, dst, slot, dev):
        pltpu.make_async_remote_copy(
            src_ref=dst, dst_ref=dst, send_sem=self.send_sem.at[slot], recv_sem=self.recv_sem.at[slot],
            device_id=dev, device_id_type=pl.DeviceIdType.MESH).wait_recv()

    def drain(self):
        for copy in self.sent:
            copy.wait_send()


def kernel(upto, tok, gain, rev, wg, wu, wd, out,
           X, XG, W, WD, F, GN, RV, snd, own, crecv, fwdp, fwdm, dirp, dirm, ysnd, yrecv, tot, H,
           D, upb, dnb, tsum, tbf, yb, SS, SSr, S2, S2r, TRI, SPR,
           XF, C, G2, c2r, x2r, H2, PF, zr, z3, yex, ZA, D2, upb2, dnb2, tsum2, tbf2, yb2, st,
           wsem, send_sem, recv_sem):
    s, t = lax.axis_index("section"), lax.axis_index("tp")
    c, x, yl = s % 2, (s // 2) % 4, s // 8
    z, yh = t // 4, t % 4
    wire = Wire(send_sem, recv_sem)
    mine, other = yl, 1 - yl

    def sec(dc=0, dx=0, dy=0):
        return ((((yl + dy + 2) % 2) * 4 + (x + dx + 4) % 4) * 2 + (c + dc) % 2, t)

    def tpd(dz=0, dh=0):
        return (s, ((z + dz + 8) % 8) * 4 + (yh + dh + 4) % 4)

    core, ydev = sec(dc=1), sec(dy=1)
    xs = {j: sec(dx=j) for j in (1, 2, 3)}
    zs = {j: tpd(dz=j) for j in range(1, 8)}
    ups, downs = zs[1], zs[7]
    yhs = {j: tpd(dh=j) for j in (1, 2, 3)}
    around = [(2, 1), (2, 0), (1, 1), (3, 1), (1, 0), (3, 0), (0, 1)]
    xys = [sec(dx=a, dy=b) for a, b in around]

    loads = []
    for g, (lo, w) in enumerate(GROUPS):
        loads.append(pltpu.make_async_copy(wg.at[:, lo:lo + w], W.at[:, 2 * lo:2 * lo + w], wsem.at[2 * g]))
        loads.append(pltpu.make_async_copy(wu.at[:, lo:lo + w], W.at[:, 2 * lo + w:2 * lo + 2 * w], wsem.at[2 * g + 1]))
    load_down = pltpu.make_async_copy(wd, WD, wsem.at[8])
    my_rows = pl.ds(mo(t * 16, 16), 16)
    small = [pltpu.make_async_copy(tok, X.at[my_rows, :], wsem.at[9]), pltpu.make_async_copy(rev, RV, wsem.at[10]),
             pltpu.make_async_copy(gain, GN, wsem.at[11])]
    for load in small + loads + [load_down]:
        load.start()

    barrier = pltpu.get_barrier_semaphore()
    peers = [core] + list(zs.values()) + list(yhs.values()) + xys
    for peer in peers:
        pl.semaphore_signal(barrier, inc=1, device_id=peer, device_id_type=pl.DeviceIdType.MESH)
    TRI[...] = jnp.where(lax.broadcasted_iota(jnp.int32, (512, 512), 0)
                         <= lax.broadcasted_iota(jnp.int32, (512, 512), 1), 1.0, 0.0).astype(BF)
    SPR[...] = jnp.where(lax.broadcasted_iota(jnp.int32, (128, 512), 1) % 16
                         == lax.broadcasted_iota(jnp.int32, (128, 512), 0), 1.0, 0.0).astype(BF)
    for load in small:
        load.wait()
    flag_row = jnp.where(RV[...] == 2, 1.0, 0.0)
    F[t] = jnp.concatenate([flag_row, jnp.zeros((1, 112), F32)], axis=1)
    pl.semaphore_wait(barrier, len(peers))
    done = object()

    def finish():
        wire.drain()

    def rows(dz, j):
        return X.at[pl.ds(mo(((z + dz + 8) % 8) * 64 + ((yh - j + 4) % 4) * 16, 16), 16), :]

    def frow(dz):
        return F.at[pl.ds(((z + dz + 8) % 8) * 4, 4)]

    def same(ref, slot, dev):
        wire.send(ref, ref, slot, dev)

    fy = {j: wire.slot() for j in (1, 2, 3)}
    fz = {d: wire.slot() for d in range(1, 8)}
    sy = {j: wire.slot() for j in (1, 2, 3)}
    sz = {(d, j): wire.slot() for d in range(1, 8) for j in range(4)}
    for j in (2, 1, 3):
        same(F.at[pl.ds(t, 1)], fy[j], yhs[j])
        same(rows(0, 0), sy[j], yhs[j])

    def spread(j):
        for d in (2, 6, 1, 7):
            same(rows(0, j), sz[d, j], zs[d])

    def relay(j):
        wire.recv(rows(-2, j), sz[2, j], zs[6])
        if j in (0, 1):
            same(rows(-2, j), sz[4, j], zs[2])
        same(rows(-2, j), sz[3, j], zs[1])
        wire.recv(rows(2, j), sz[6, j], zs[2])
        if j in (2, 3):
            same(rows(2, j), sz[4, j], zs[6])
        same(rows(2, j), sz[5, j], zs[7])

    def take(j):
        wire.recv(rows(-1, j), sz[1, j], zs[7])
        wire.recv(rows(1, j), sz[7, j], zs[1])
        wire.recv(rows(-3, j), sz[3, j], zs[7])
        wire.recv(rows(3, j), sz[5, j], zs[1])
        wire.recv(rows(4, j), sz[4, j], zs[6] if j in (0, 1) else zs[2])

    spread(0)
    for j in (1, 3):
        wire.recv(rows(0, j), sy[j], yhs[4 - j])
        spread(j)
    relay(0)
    for j in (1, 2, 3):
        wire.recv(F.at[pl.ds(z * 4 + (yh - j + 4) % 4, 1)], fy[j], yhs[4 - j])
    for d in (2, 6, 1, 7):
        same(frow(0), fz[d], zs[d])
    wire.recv(rows(0, 2), sy[2], yhs[2])
    spread(2)
    relay(1)
    relay(3)
    wire.recv(frow(-2), fz[2], zs[6])
    same(frow(-2), fz[4], zs[2])
    same(frow(-2), fz[3], zs[1])
    wire.recv(frow(2), fz[6], zs[2])
    same(frow(2), fz[5], zs[7])
    relay(2)
    wire.recv(frow(-1), fz[1], zs[7])
    wire.recv(frow(1), fz[7], zs[1])
    wire.recv(frow(-3), fz[3], zs[7])
    wire.recv(frow(3), fz[5], zs[1])
    wire.recv(frow(4), fz[4], zs[6])
    for j in (0, 1, 3, 2):
        take(j)
    if upto < 1:
        for load in loads + [load_down]:
            load.wait()
        out[...] = X[my_rows, :]
        return finish()

    flags = F[...].reshape(32, 128)
    lanes = jnp.dot(flags.astype(BF), SPR[...], preferred_element_type=F32)
    owner = lax.broadcasted_iota(jnp.int32, (32, 512), 1) // 16
    unit = lax.broadcasted_iota(jnp.int32, (32, 512), 0)
    active = jnp.sum(jnp.where(unit == owner, lanes, 0.0), axis=0, keepdims=True)
    upto_here = jnp.dot(jnp.broadcast_to(active, (16, 512)).astype(BF), TRI[...], preferred_element_type=F32)[0:1, :]
    want = lax.broadcasted_iota(jnp.int32, (64, 512), 0).astype(F32)
    goal = jnp.where(active > 0.5, upto_here - 1.0, -1.0)
    choose = jnp.where(goal == want, 1.0, 0.0).astype(BF)
    g = GN[...]
    XF[...] = jnp.dot(choose, X[...], preferred_element_type=F32)
    NG = len(GROUPS)

    def cols(p):
        lo, w = GROUPS[p]
        return slice(2 * lo, 2 * lo + 2 * w)

    def sq_rounds(ss, rr):
        slots = [wire.slot() for _ in range(8)]
        wire.send(ss, rr.at[0], slots[0], core)
        yield
        wire.recv(rr.at[0], slots[0], core)
        rr[8] = ss[...] + rr[0]
        for q in range(7):
            wire.send(rr.at[8], rr.at[q + 1], slots[q + 1], xys[q])
        yield
        total = rr[8]
        for q in range(7):
            wire.recv(rr.at[q + 1], slots[q + 1], sec(dx=-around[q][0], dy=around[q][1]))
            total = total + rr[q + 1]
        rr[9] = total
        yield

    def scale_of(rr, first, count):
        line = rr[9, pl.ds(first // 128, 1), :]
        picked = jnp.where(eye(count, 128, first % 128), line, 0.0)
        return lax.rsqrt(jnp.sum(picked, axis=1, keepdims=True) / FEATURES + EPS)

    def act(gate, up):
        return (gate / (1.0 + jnp.exp(-gate)) * up).astype(BF)

    def packed(n):
        v = XF[...]
        C[n] = (v * g).astype(BF)
        col = jnp.sum(v * v, axis=1, keepdims=True)
        s2 = S2.at[n]
        s2[...] = jnp.zeros((8, 128), F32)
        s2[0:1, :] = jnp.sum(jnp.where(eye(64, 128), col, 0.0), axis=0, keepdims=True)
        g2, h2all = G2.at[n], H2.at[n]
        for p in range(NG):
            if n == 0:
                loads[2 * p].wait()
                loads[2 * p + 1].wait()
            lo, w = GROUPS[p]
            prod = jnp.dot(C[n], W[:, cols(p)], preferred_element_type=F32).astype(BF)
            g2[:, 512 * p:512 * p + w] = prod[:, 0:w]
            g2[:, 512 * p + 256:512 * p + 256 + w] = prod[:, w:2 * w]
            if w < 256:
                g2[:, 512 * p + w:512 * p + 256] = jnp.zeros((64, 256 - w), BF)
                g2[:, 512 * p + 256 + w:512 * p + 512] = jnp.zeros((64, 256 - w), BF)
        slot = wire.slot()
        wire.send(g2.at[pl.ds(mo((1 - c) * 32, 32), 32), :], c2r.at[n], slot, core)
        sq = sq_rounds(s2, S2r.at[n])
        next(sq)
        yield
        core_rows = pl.ds(mo(c * 32, 32), 32)
        wire.recv(c2r.at[n], slot, core)
        g2[core_rows, :] = (g2[core_rows, :].astype(F32) + c2r[n].astype(F32)).astype(BF)

        def block(dx, dy):
            return g2.at[pl.ds(mo(c * 32 + ((yl + dy) % 2) * 16, 16), 16), pl.ds(mo(((x + dx) % 4) * 512, 512), 512)]
        slots = [wire.slot() for _ in range(7)]
        for q, (dx, dy) in enumerate(around):
            wire.send(block(dx, dy), x2r.at[n, q], slots[q], xys[q])
        next(sq)
        yield
        total = block(0, 0)[...].astype(F32)
        for q, (dx, dy) in enumerate(around):
            wire.recv(x2r.at[n, q], slots[q], sec(dx=-dx, dy=dy))
            total = total + x2r[n, q].astype(F32)
        next(sq)
        total = total * scale_of(S2r.at[n], c * 32 + yl * 16, 16)

        def hid(dx, dy):
            return h2all.at[pl.ds(mo(c * 32 + ((yl + dy) % 2) * 16, 16), 16), pl.ds(mo(((x + dx + 4) % 4) * 256, 256), 256)]
        hid(0, 0)[...] = act(total[:, 0:256], total[:, 256:512])
        slots = [wire.slot() for _ in range(7)]
        for q in range(7):
            same(hid(0, 0), slots[q], xys[q])
        yield
        for q, (dx, dy) in enumerate(around):
            wire.recv(hid(-dx, dy), slots[q], sec(dx=-dx, dy=dy))
        slot = wire.slot()
        same(h2all.at[core_rows, :], slot, core)
        yield
        wire.recv(h2all.at[pl.ds(mo((1 - c) * 32, 32), 32), :], slot, core)
        yield

    def all_sum(prod):
        folded = jnp.concatenate([prod[:, 0:256].reshape(8, 8, 256), prod[:, 256:512].reshape(8, 8, 256)], axis=1)
        PF[...] = folded.reshape(128, 256).astype(BF)

        def blk16(ref, dz):
            return ref.at[pl.ds(mo(((z + dz + 8) % 8) * 16, 16), 16), :]
        slots = {d: wire.slot() for d in range(1, 8)}
        for d in (4, 3, 5, 2, 6, 1, 7):
            wire.send(blk16(PF, d), zr.at[d - 1], slots[d], zs[d])
        yield
        total = blk16(PF, 0)[...].astype(F32)
        for d in (1, 7, 2, 6, 3, 5, 4):
            wire.recv(zr.at[d - 1], slots[d], zs[8 - d])
            total = total + zr[d - 1].astype(F32)
        yex[...] = total.astype(BF)
        ys = {j: wire.slot() for j in (1, 2, 3)}
        for j in (2, 1, 3):
            wire.send(yex, z3.at[j - 1], ys[j], yhs[j])
        yield
        for j in (1, 3, 2):
            wire.recv(z3.at[j - 1], ys[j], yhs[4 - j])
            total = total + z3[j - 1].astype(F32)
        blk16(ZA, 0)[...] = total.astype(BF)
        zg = {d: wire.slot() for d in range(1, 8)}
        for d in (4, 3, 5, 2, 6, 1, 7):
            same(blk16(ZA, 0), zg[d], zs[d])
        yield
        for d in (1, 7, 2, 6, 3, 5, 4):
            wire.recv(blk16(ZA, -d), zg[d], zs[8 - d])
        got = ZA[...].astype(F32).reshape(8, 16, 256)
        change = jnp.concatenate([got[:, 0:8, :].reshape(64, 256), got[:, 8:16, :].reshape(64, 256)], axis=1)
        XF[...] = XF[...] + change
        yield

    def ring_reduce(src, ub, db, ts, tb, ybuf, result, block_done):
        def part(off, h):
            return src.at[pl.ds(mo(((z + off + 8) % 8) * 64 + h * 32, 32), 32), :]

        us = {(k, h): wire.slot() for k in range(4) for h in range(2)}
        ds = {(k, h): wire.slot() for k in range(4) for h in range(2)}
        block_done(4)
        wire.send(part(4, 0), ub.at[0, 0:32, :], us[0, 0], ups)
        wire.send(part(4, 1), db.at[0, 32:64, :], ds[0, 1], downs)
        for k in (1, 2, 3):
            block_done(4 - k)
            yield
            for h in ((1, 0) if k == 1 else (0, 1)):
                hu, hd = h, 1 - h
                if k > 1 or hu == 0:
                    got = ub.at[k - 1, hu * 32:hu * 32 + 32, :]
                    wire.recv(got, us[k - 1, hu], downs)
                    acc = part(4 - k, hu)
                    acc[...] = (acc[...].astype(F32) + got[...].astype(F32)).astype(BF)
                wire.send(part(4 - k, hu), ub.at[k, hu * 32:hu * 32 + 32, :], us[k, hu], ups)
                if k > 1 or hd == 1:
                    got = db.at[k - 1, hd * 32:hd * 32 + 32, :]
                    wire.recv(got, ds[k - 1, hd], ups)
                    acc = part(k - 4, hd)
                    acc[...] = (acc[...].astype(F32) + got[...].astype(F32)).astype(BF)
                wire.send(part(k - 4, hd), db.at[k, hd * 32:hd * 32 + 32, :], ds[k, hd], downs)
        yield
        for h in (0, 1):
            a, b = ub.at[3, h * 32:h * 32 + 32, :], db.at[3, h * 32:h * 32 + 32, :]
            wire.recv(a, us[3, h], downs)
            wire.recv(b, ds[3, h], ups)
            total = part(0, h)[...].astype(F32) + a[...].astype(F32) + b[...].astype(F32)
            ts[h * 32:h * 32 + 32, :] = total
            tb[h * 32:h * 32 + 32, :] = total.astype(BF)
        ys = {j: wire.slot() for j in (1, 2, 3)}
        for j in (2, 1, 3):
            wire.send(tb.at[pl.ds(mo(((yh + j) % 4) * 16, 16), 16), :], ybuf.at[j - 1], ys[j], yhs[j])
        yield
        total = ts[pl.ds(mo(yh * 16, 16), 16), :]
        for j in (1, 3, 2):
            wire.recv(ybuf.at[j - 1], ys[j], yhs[4 - j])
            total = total + ybuf[j - 1].astype(F32)
        result.append(total)
        yield

    def bulk():
        for b in range(4):
            part_cols = []
            for q in range(4):
                lo = b * 128 + q * 32
                v = X[lo:lo + 32, :].astype(F32)
                XG[lo:lo + 32, :] = (v * g).astype(BF)
                part_cols.append(jnp.sum(v * v, axis=1, keepdims=True))
            col = jnp.concatenate(part_cols, axis=0)
            SS[b:b + 1, :] = jnp.sum(jnp.where(eye(128, 128), col, 0.0), axis=0, keepdims=True)
        SS[4:8, :] = jnp.zeros((4, 128), F32)

        def gate_up(row0, p, dst):
            @pl.loop(0, 2)
            def _(i):
                r = mo(i * 128, 128)
                dst[pl.ds(r, 128), cols(p)] = jnp.dot(
                    XG[pl.ds(mo(row0 + r, 128), 128), :], W[:, cols(p)],
                    preferred_element_type=F32).astype(BF)

        cslot = [wire.slot() for _ in range(NG)]
        for p in range(NG):
            gate_up((1 - c) * 256, p, snd)
            wire.send(snd.at[:, cols(p)], crecv.at[:, cols(p)], cslot[p], core)
        sq = sq_rounds(SS, SSr)
        next(sq)
        yield
        for p in range(NG):
            gate_up(c * 256, p, own)
        yield

        def blk(off, h):
            return pl.ds(mo(((x + off) % 4) * 64 + h * 32, 32), 32)

        xslot = [[wire.slot() for _ in range(6)] for _ in range(NG)]
        for p in range(NG):
            wire.recv(crecv.at[:, cols(p)], cslot[p], core)

            @pl.loop(0, 8)
            def _(i):
                r = pl.ds(mo(i * 32, 32), 32)
                own[r, cols(p)] = (own[r, cols(p)].astype(F32) + crecv[r, cols(p)].astype(F32)).astype(BF)
            wire.send(own.at[blk(2, 0), cols(p)], fwdp.at[:, cols(p)], xslot[p][0], xs[1])
            wire.send(own.at[blk(2, 1), cols(p)], fwdm.at[:, cols(p)], xslot[p][1], xs[3])
            wire.send(own.at[blk(1, 1), cols(p)], dirp.at[32:64, cols(p)], xslot[p][2], xs[1])
            wire.send(own.at[blk(3, 0), cols(p)], dirm.at[0:32, cols(p)], xslot[p][3], xs[3])
        next(sq)
        yield
        for p in range(NG):
            wire.recv(fwdp.at[:, cols(p)], xslot[p][0], xs[3])
            r = blk(1, 0)
            own[r, cols(p)] = (own[r, cols(p)].astype(F32) + fwdp[:, cols(p)].astype(F32)).astype(BF)
            wire.send(own.at[r, cols(p)], dirp.at[0:32, cols(p)], xslot[p][4], xs[1])
            wire.recv(fwdm.at[:, cols(p)], xslot[p][1], xs[1])
            r = blk(3, 1)
            own[r, cols(p)] = (own[r, cols(p)].astype(F32) + fwdm[:, cols(p)].astype(F32)).astype(BF)
            wire.send(own.at[r, cols(p)], dirm.at[32:64, cols(p)], xslot[p][5], xs[3])
        next(sq)
        yield
        yslot = [wire.slot() for _ in range(NG)]
        for p in range(NG):
            wire.recv(dirp.at[32:64, cols(p)], xslot[p][2], xs[3])
            wire.recv(dirm.at[0:32, cols(p)], xslot[p][3], xs[1])
            wire.recv(dirp.at[0:32, cols(p)], xslot[p][4], xs[3])
            wire.recv(dirm.at[32:64, cols(p)], xslot[p][5], xs[1])

            def xsum(h):
                hr = pl.ds(mo(h * 32, 32), 32)
                return (own[blk(0, h), cols(p)].astype(F32) + dirp[hr, cols(p)].astype(F32)
                        + dirm[hr, cols(p)].astype(F32))
            ysnd[:, cols(p)] = xsum(other).astype(BF)
            wire.send(ysnd.at[:, cols(p)], yrecv.at[:, cols(p)], yslot[p], ydev)
            tot[:, cols(p)] = xsum(mine)
        yield
        scale = scale_of(SSr, c * 256 + x * 64 + yl * 32, 32)

        def hrows(off, h):
            return pl.ds(mo(c * 256 + ((x + off) % 4) * 64 + h * 32, 32), 32)

        hy = [wire.slot() for _ in range(NG)]
        hx = [[wire.slot() for _ in range(6)] for _ in range(NG)]
        hc = [wire.slot() for _ in range(NG)]

        def hcols(p):
            lo, w = GROUPS[p]
            return slice(lo, lo + w)

        def hsend(off, h, p, slot, dev):
            same(H.at[hrows(off, h), hcols(p)], slot, dev)

        def hrecv(off, h, p, slot, dev):
            wire.recv(H.at[hrows(off, h), hcols(p)], slot, dev)

        for p in range(NG):
            lo, w = GROUPS[p]
            wire.recv(yrecv.at[:, cols(p)], yslot[p], ydev)
            gate = (tot[:, 2 * lo:2 * lo + w] + yrecv[:, 2 * lo:2 * lo + w].astype(F32)) * scale
            up = (tot[:, 2 * lo + w:2 * lo + 2 * w] + yrecv[:, 2 * lo + w:2 * lo + 2 * w].astype(F32)) * scale
            H[hrows(0, mine), hcols(p)] = act(gate, up)
            hsend(0, mine, p, hy[p], ydev)
            hsend(0, mine, p, hx[p][0], xs[1])
            hsend(0, mine, p, hx[p][1], xs[3])
        yield
        for p in range(NG):
            hrecv(0, other, p, hy[p], ydev)
            hsend(0, other, p, hx[p][2], xs[1])
            hsend(0, other, p, hx[p][3], xs[3])
            hrecv(3, mine, p, hx[p][0], xs[3])
            hsend(3, mine, p, hx[p][4], xs[1])
            hrecv(1, mine, p, hx[p][1], xs[1])
        yield
        for p in range(NG):
            hrecv(3, other, p, hx[p][2], xs[3])
            hrecv(1, other, p, hx[p][3], xs[1])
            hsend(1, other, p, hx[p][5], xs[3])
        yield
        for p in range(NG):
            hrecv(2, mine, p, hx[p][4], xs[3])
            hrecv(2, other, p, hx[p][5], xs[1])
            half = H.at[pl.ds(mo(c * 256, 256), 256), hcols(p)]
            same(half, hc[p], core)
        yield
        for p in range(NG):
            wire.recv(H.at[pl.ds(mo((1 - c) * 256, 256), 256), hcols(p)], hc[p], core)

        def down_pair(off):
            a = pl.ds(mo(((z + off) % 8) * 64, 64), 64)
            b = pl.ds(mo(((z - off + 8) % 8) * 64, 64), 64)
            if off == 4:
                b = pl.ds(mo(z * 64, 64), 64)
            both = jnp.concatenate([H[a, :], H[b, :]], axis=0)
            prod = jnp.dot(both, WD[...], preferred_element_type=F32).astype(BF)
            D[a, :] = prod[0:64]
            D[b, :] = prod[64:128]

        delta = []
        for _ in ring_reduce(D, upb, dnb, tsum, tbf, yb, delta, down_pair):
            if not delta:
                yield
        st[...] = tok_rows() + delta[0]
        yield

    def tok_rows():
        return X[my_rows, :].astype(F32)

    def down_of(n):
        return jnp.dot(H2[n, :, 0:896], WD[...], preferred_element_type=F32)

    def run(*gens):
        for gen in gens:
            next(gen)

    p1, big = packed(0), bulk()

    def stop(*gens):
        for gen in gens:
            for _ in gen:
                pass
        load_down.wait()
        out[...] = XF[0:16, :].astype(BF)
        finish()

    run(p1)
    run(p1, big)
    run(big)
    run(p1)
    run(p1)
    run(p1)
    load_down.wait()
    if upto < 2:
        return stop(big)
    total = all_sum(down_of(0))
    run(total)
    run(big)
    run(total)
    run(big)
    run(total)
    run(big)
    run(total)
    if upto < 3:
        return stop(big)
    p2 = packed(1)
    run(p2)
    run(big)
    run(p2)
    run(big)
    run(p2)
    run(big)
    run(p2)
    run(big, p2)
    run(big)

    down2 = down_of(1).astype(BF)
    counts = jnp.sum(flags, axis=1, keepdims=True)
    before = jnp.sum(jnp.where(unit < owner, counts, 0.0), axis=0, keepdims=True)
    here = jnp.sum(jnp.where(unit == owner, counts, 0.0), axis=0, keepdims=True)
    slot_lane = lax.broadcasted_iota(jnp.int32, (1, 512), 1) % 16
    place = (slot_lane % 8).astype(F32)
    goal = jnp.where(place < here, before + place, -1.0)
    hit = jnp.where(goal == want, 1.0, 0.0)
    left = jnp.where(slot_lane < 8, hit, 0.0).astype(BF)
    right = jnp.where(slot_lane >= 8, hit, 0.0).astype(BF)
    dims = (((0,), (0,)), ((), ()))
    D2[...] = (lax.dot_general(left, down2[:, 0:256], dims, preferred_element_type=F32)
               + lax.dot_general(right, down2[:, 256:512], dims, preferred_element_type=F32)).astype(BF)
    back = []
    last = ring_reduce(D2, upb2, dnb2, tsum2, tbf2, yb2, back, lambda off: None)

    for k in range(6):
        run(last)
        if k < 5:
            for _ in range(1 if k else 2):
                if next(big, done) is done:
                    break
    for _ in big:
        pass
    back = back[0]
    act_row = (RV[...] == 2).astype(F32)
    sub = lax.broadcasted_iota(jnp.int32, (16, 16), 0)
    lane = lax.broadcasted_iota(jnp.int32, (16, 16), 1)
    act_col = jnp.sum(jnp.where(sub == lane, act_row, 0.0), axis=1, keepdims=True)
    place_col = jnp.sum(jnp.where(lane <= sub, act_row, 0.0), axis=1, keepdims=True) - 1.0
    acc_l = jnp.zeros((16, 256), F32)
    acc_r = jnp.zeros((16, 256), F32)
    for k in range(8):
        put = jnp.where((place_col == k) & (act_col > 0.5), 1.0, 0.0)
        acc_l = acc_l + put * back[k:k + 1, :]
        acc_r = acc_r + put * back[k + 8:k + 9, :]
    out[...] = (st[...] + jnp.concatenate([acc_l, acc_r], axis=1)).astype(BF)
    finish()


def body(upto, tokens, norm_gain, gate_weight, up_weight, down_weight, revisit):
    vm = lambda *shape: pltpu.VMEM(shape, BF)
    vf = lambda *shape: pltpu.VMEM(shape, F32)
    vspec, hbm = pl.BlockSpec(memory_space=pltpu.VMEM), pl.BlockSpec(memory_space=pltpu.MemorySpace.HBM)
    scratch = [
        vm(512, 512), vm(512, 512), vm(512, 1792), vm(896, 512), vf(32, 1, 128), vf(1, 512),
        pltpu.VMEM((1, 16), jnp.int32),
        vm(256, 1792), vm(256, 1792), vm(256, 1792), vm(32, 1792), vm(32, 1792), vm(64, 1792), vm(64, 1792),
        vm(32, 1792), vm(32, 1792), vf(32, 1792), vm(512, 896),
        vm(512, 512), vm(4, 64, 512), vm(4, 64, 512), vf(64, 512), vm(64, 512), vm(3, 16, 512),
        vf(8, 128), vf(10, 8, 128), vf(2, 8, 128), vf(2, 10, 8, 128), vm(512, 512), vm(128, 512),
        vf(64, 512), vm(2, 64, 512), vm(2, 64, 2048), vm(2, 32, 2048), vm(2, 7, 16, 512), vm(2, 64, 1024),
        vm(128, 256), vm(7, 16, 256), vm(3, 16, 256), vm(16, 256), vm(128, 256),
        vm(512, 256), vm(4, 64, 256), vm(4, 64, 256), vf(64, 256), vm(64, 256), vm(3, 16, 256),
        vf(16, 512),
        pltpu.SemaphoreType.DMA((12,)), pltpu.SemaphoreType.DMA((320,)), pltpu.SemaphoreType.DMA((320,)),
    ]
    return pl.pallas_call(
        functools.partial(kernel, upto),
        out_shape=jax.ShapeDtypeStruct((16, 512), BF),
        in_specs=[hbm] * 6,
        out_specs=vspec,
        scratch_shapes=scratch,
        compiler_params=pltpu.CompilerParams(
            collective_id=0, has_side_effects=True, vmem_limit_bytes=40 * 1024 * 1024),
        cost_estimate=pl.CostEstimate(flops=2000000000, bytes_accessed=3000000, transcendentals=30000),
        name="two_pass_block",
    )(tokens, norm_gain.reshape(1, 512), revisit.reshape(1, 16), gate_weight, up_weight, down_weight)


def solution(mesh, upto=LAST):
    placed = (P("tp", "section"), P("section"), P("section", "tp"), P("section", "tp"), P("tp", "section"), P("tp"))
    return jax.shard_map(functools.partial(body, upto), mesh=mesh, in_specs=placed,
                         out_specs=P("tp", "section"), check_vma=False)
```

time: 955 us -> 101 us (0.11)
  waiting for transfers between devices: 718 us -> 0 us
  blocking collectives: 203 us -> 0 us
  Pallas kernels: 0 us -> 93.7 us
  matrix products: 13.6 us -> 0 us
  between operations: 13.2 us -> 0.02 us
    reduce_scatter x2 -> x0, waiting for transfers between devices: 446 us -> none  [the longest x1 223 us: body(): lax.psum_scatter(partial_value.astype(jnp.bfloat16), 'tp', scatter_dimens...]
    psum x2 -> x0, waiting for transfers between devices: 272 us -> none  [project(): lax.psum(up_part.astype(jnp.bfloat16), 'section').astype(jnp.float32)]
    all_gather x2 -> x0, blocking collectives: 138 us -> none  [the longest x1 71.5 us: body(): gathered = lax.all_gather(first_normed, 'tp', axis=0, tiled=True)]
    pallas_call x0 -> x1, Pallas kernels: none -> 93.7 us  [body(): pl.pallas_call(functools.partial(kernel, upto), out_shape=jax.ShapeDtypeS...]
    psum x2 -> x0, blocking collectives: 65 us -> none  [normalize(): summed_sq = lax.psum(squares, 'section')]
    dot_general x8 -> x0, matrix products: 13.6 us -> none  [the longest x2 5.45 us: project(): return jnp.dot(hidden, down_weight, preferred_element_type=jnp.float32)]
  transfers between devices with their start and end apart: 4 -> 0, of which waited for: 4 -> 0; matrix products, arithmetic and copies ran while one was open for 0% -> 0% of each run, Pallas kernels for 0% -> 0%
where the time goes in v2:
time: 101 us; the launch traced here: 99.3 us
  Pallas kernels  93.7 us (93%)
  local copies, waits for them, and re-layouts  5.54 us (5%)
    pallas_call x1, Pallas kernels, body(): pl.pallas_call(functools.partial(kernel, upto), out_shape=jax.ShapeDtypeS...  93.7 us
    unnamed x13, local copies, waits for them, and re-layouts  5.54 us

profile of v2, /device:TPU:1, one launch (start us, length us, event | category | flops | bytes accessed | tf_op | source)
XLA Modules:
  0.0 99.3 jit_solution(16406267346460327080)
XLA Ops:
  0.0 0.0 copy-start.4
  0.0 0.0 copy-start.5
  0.0 0.7 copy-done.4
  0.7 0.0 copy-done.5
  0.7 0.0 copy-start
  0.7 1.2 %copy-done = bf16[512,896]{1,0:T(8,128)(2,1)S(1)} copy-done((bf16[512,896]{1,0:T(8,128)(2,1)S(1)}, bf16[512,896]{1,0:T(8,128)(2,1)}, u32[]{:S(2)}) %copy-start) | copy-done | bytes 917528
  1.9 0.0 copy-start.1
  1.9 1.2 %copy-done.1 = bf16[512,896]{1,0:T(8,128)(2,1)S(1)} copy-done((bf16[512,896]{1,0:T(8,128)(2,1)S(1)}, bf16[512,896]{1,0:T(8,128)(2,1)}, u32[]{:S(2)}) %copy-start.1) | copy-done | bytes 917528
  3.0 0.0 copy-start.2
  3.0 1.2 %copy-done.2 = bf16[896,512]{1,0:T(8,128)(2,1)S(1)} copy-done((bf16[896,512]{1,0:T(8,128)(2,1)S(1)}, bf16[896,512]{1,0:T(8,128)(2,1)}, u32[]{:S(2)}) %copy-start.2) | copy-done | bytes 917528
  4.2 0.0 copy-start.3
  4.2 0.7 copy-done.3
  4.9 93.7 %two_pass_block.1 = bf16[16,512]{1,0:T(8,128)(2,1)S(1)} custom-call(bf16[16,512]{1,0:T(8,128)(2,1)S(1)} %copy-done.3, f32[1,512]{1,0:T(1,128)S(1)} %bitcast.2, s32[1,16]{1,0:T(1,128)S(1)} %bitcast.3, bf16[512,896]{1,0:T(8,128)(2,1)S(1)} %copy-done, bf16[512,896]{1,0:T(8,128)(2,1)S(1)} %copy-done.1, bf16[896,512]{1,0:T(8,128)(2,1)S(1)} %copy-done.2), custom_call_target="tpu_custom_call" | custom-call | flops 2000000000 | bytes 3000000 | tf_op jit(solution)/shard_map/two_pass_block/pallas_call | solution.py:602
  98.7 0.6 copy.8
Async XLA Ops:
  0.0 0.7 copy-start.4
  0.0 0.7 copy-start.5
  0.7 1.2 %copy-start = (bf16[512,896]{1,0:T(8,128)(2,1)S(1)}, bf16[512,896]{1,0:T(8,128)(2,1)}, u32[]{:S(2)}) copy-start(bf16[512,896]{1,0:T(8,128)(2,1)} %wg.1) | copy-start | bytes 2752516
  1.9 1.2 %copy-start.1 = (bf16[512,896]{1,0:T(8,128)(2,1)S(1)}, bf16[512,896]{1,0:T(8,128)(2,1)}, u32[]{:S(2)}) copy-start(bf16[512,896]{1,0:T(8,128)(2,1)} %wu.1) | copy-start | bytes 2752516
  3.0 1.2 %copy-start.2 = (bf16[896,512]{1,0:T(8,128)(2,1)S(1)}, bf16[896,512]{1,0:T(8,128)(2,1)}, u32[]{:S(2)}) copy-start(bf16[896,512]{1,0:T(8,128)(2,1)} %wd.1) | copy-start | bytes 2752516
  4.2 0.7 copy-start.3

commit v3 on v2

--- a/solution.py
+++ b/solution.py
@@ -50,9 +50,9 @@
 
 
 def kernel(upto, tok, gain, rev, wg, wu, wd, out,
-           X, XG, W, WD, F, GN, RV, snd, own, crecv, fwdp, fwdm, dirp, dirm, ysnd, yrecv, tot, H,
-           D, upb, dnb, tsum, tbf, yb, SS, SSr, S2, S2r, TRI, SPR,
-           XF, C, G2, c2r, x2r, H2, PF, zr, z3, yex, ZA, D2, upb2, dnb2, tsum2, tbf2, yb2, st,
+           X, W, WD, F, GN, RV, G, own, crecv, fwdp, fwdm, dirp, dirm, ysnd, yrecv, tot, H,
+           D, q4, q3, n1, n2, tsum, tbf, yb, SS, SSr, S2, S2r, TRI, SPR,
+           XF, C, G2, c2r, x2r, H2, PF, zr, z3, yex, ZA, st,
            wsem, send_sem, recv_sem):
     s, t = lax.axis_index("section"), lax.axis_index("tp")
     c, x, yl = s % 2, (s // 2) % 4, s // 8
@@ -134,12 +134,43 @@
             same(rows(2, j), sz[4, j], zs[6])
         same(rows(2, j), sz[5, j], zs[7])
 
-    def take(j):
-        wire.recv(rows(-1, j), sz[1, j], zs[7])
-        wire.recv(rows(1, j), sz[7, j], zs[1])
-        wire.recv(rows(-3, j), sz[3, j], zs[7])
-        wire.recv(rows(3, j), sz[5, j], zs[1])
-        wire.recv(rows(4, j), sz[4, j], zs[6] if j in (0, 1) else zs[2])
+    def take(d):
+        for j in (0, 1, 3, 2):
+            if d == 4:
+                wire.recv(rows(4, j), sz[4, j], zs[6] if j in (0, 1) else zs[2])
+            else:
+                wire.recv(rows(-d, j), sz[d, j], zs[7])
+                wire.recv(rows(d, j), sz[8 - d, j], zs[1])
+
+    NG = len(GROUPS)
+
+    def cols(p):
+        lo, w = GROUPS[p]
+        return slice(2 * lo, 2 * lo + 2 * w)
+
+    cslot = {d: wire.slot() for d in range(8)}
+    g = GN[...]
+
+    def half_rows(d, cc):
+        return pl.ds(mo(((z + d) % 8) * 64 + cc * 32, 32), 32)
+
+    def unit_rows(d):
+        return pl.ds(mo(((z + d) % 8) * 32, 32), 32)
+
+    def gate_up(ds):
+        blocks = [pl.ds(mo(((z + d) % 8) * 64, 64), 64) for d in ds]
+        v = jnp.concatenate([X[b, :] for b in blocks], axis=0).astype(F32)
+        scaled = (v * g).astype(BF)
+        col = jnp.sum(v * v, axis=1, keepdims=True)
+        for n, d in enumerate(ds):
+            SS[pl.ds((z + d) % 8, 1), :] = jnp.sum(
+                jnp.where(eye(64, 128), col[n * 64:n * 64 + 64], 0.0), axis=0, keepdims=True)
+        for p in range(NG):
+            prod = jnp.dot(scaled, W[:, cols(p)], preferred_element_type=F32).astype(BF)
+            for n, b in enumerate(blocks):
+                G[b, cols(p)] = prod[n * 64:n * 64 + 64]
+        for d in ds:
+            wire.send(G.at[half_rows(d, 1 - c), :], crecv.at[unit_rows(d), :], cslot[d], core)
 
     spread(0)
     for j in (1, 3):
@@ -154,22 +185,29 @@
     spread(2)
     relay(1)
     relay(3)
+    for load in loads:
+        load.wait()
+    if upto not in (0, 7, 70, 71, 72):
+        gate_up((0,))
     wire.recv(frow(-2), fz[2], zs[6])
     same(frow(-2), fz[4], zs[2])
     same(frow(-2), fz[3], zs[1])
     wire.recv(frow(2), fz[6], zs[2])
     same(frow(2), fz[5], zs[7])
     relay(2)
+    take(1)
+    if upto not in (0, 7, 70, 71, 72):
+        gate_up((1, 7))
+        gate_up((2, 6))
     wire.recv(frow(-1), fz[1], zs[7])
     wire.recv(frow(1), fz[7], zs[1])
     wire.recv(frow(-3), fz[3], zs[7])
     wire.recv(frow(3), fz[5], zs[1])
     wire.recv(frow(4), fz[4], zs[6])
-    for j in (0, 1, 3, 2):
-        take(j)
+    take(3)
+    take(4)
     if upto < 1:
-        for load in loads + [load_down]:
-            load.wait()
+        load_down.wait()
         out[...] = X[my_rows, :]
         return finish()
 
@@ -182,13 +220,7 @@
     want = lax.broadcasted_iota(jnp.int32, (64, 512), 0).astype(F32)
     goal = jnp.where(active > 0.5, upto_here - 1.0, -1.0)
     choose = jnp.where(goal == want, 1.0, 0.0).astype(BF)
-    g = GN[...]
     XF[...] = jnp.dot(choose, X[...], preferred_element_type=F32)
-    NG = len(GROUPS)
-
-    def cols(p):
-        lo, w = GROUPS[p]
-        return slice(2 * lo, 2 * lo + 2 * w)
 
     def sq_rounds(ss, rr):
         slots = [wire.slot() for _ in range(8)]
@@ -223,9 +255,6 @@
         s2[0:1, :] = jnp.sum(jnp.where(eye(64, 128), col, 0.0), axis=0, keepdims=True)
         g2, h2all = G2.at[n], H2.at[n]
         for p in range(NG):
-            if n == 0:
-                loads[2 * p].wait()
-                loads[2 * p + 1].wait()
             lo, w = GROUPS[p]
             prod = jnp.dot(C[n], W[:, cols(p)], preferred_element_type=F32).astype(BF)
             g2[:, 512 * p:512 * p + w] = prod[:, 0:w]
@@ -271,127 +300,108 @@
         wire.recv(h2all.at[pl.ds(mo((1 - c) * 32, 32), 32), :], slot, core)
         yield
 
-    def all_sum(prod):
+    def all_sum(n, prod, result):
         folded = jnp.concatenate([prod[:, 0:256].reshape(8, 8, 256), prod[:, 256:512].reshape(8, 8, 256)], axis=1)
-        PF[...] = folded.reshape(128, 256).astype(BF)
+        pf, za = PF.at[n], ZA.at[n]
+        pf[...] = folded.reshape(128, 256).astype(BF)
 
         def blk16(ref, dz):
             return ref.at[pl.ds(mo(((z + dz + 8) % 8) * 16, 16), 16), :]
         slots = {d: wire.slot() for d in range(1, 8)}
         for d in (4, 3, 5, 2, 6, 1, 7):
-            wire.send(blk16(PF, d), zr.at[d - 1], slots[d], zs[d])
-        yield
-        total = blk16(PF, 0)[...].astype(F32)
+            wire.send(blk16(pf, d), zr.at[n, d - 1], slots[d], zs[d])
+        yield
+        total = blk16(pf, 0)[...].astype(F32)
         for d in (1, 7, 2, 6, 3, 5, 4):
-            wire.recv(zr.at[d - 1], slots[d], zs[8 - d])
-            total = total + zr[d - 1].astype(F32)
-        yex[...] = total.astype(BF)
+            wire.recv(zr.at[n, d - 1], slots[d], zs[8 - d])
+            total = total + zr[n, d - 1].astype(F32)
+        yex[n] = total.astype(BF)
         ys = {j: wire.slot() for j in (1, 2, 3)}
         for j in (2, 1, 3):
-            wire.send(yex, z3.at[j - 1], ys[j], yhs[j])
-        yield
+            wire.send(yex.at[n], z3.at[n, j - 1], ys[j], yhs[j])
+        yield
+        total = yex[n].astype(F32)
         for j in (1, 3, 2):
-            wire.recv(z3.at[j - 1], ys[j], yhs[4 - j])
-            total = total + z3[j - 1].astype(F32)
-        blk16(ZA, 0)[...] = total.astype(BF)
+            wire.recv(z3.at[n, j - 1], ys[j], yhs[4 - j])
+            total = total + z3[n, j - 1].astype(F32)
+        blk16(za, 0)[...] = total.astype(BF)
         zg = {d: wire.slot() for d in range(1, 8)}
         for d in (4, 3, 5, 2, 6, 1, 7):
-            same(blk16(ZA, 0), zg[d], zs[d])
+            same(blk16(za, 0), zg[d], zs[d])
         yield
         for d in (1, 7, 2, 6, 3, 5, 4):
-            wire.recv(blk16(ZA, -d), zg[d], zs[8 - d])
-        got = ZA[...].astype(F32).reshape(8, 16, 256)
-        change = jnp.concatenate([got[:, 0:8, :].reshape(64, 256), got[:, 8:16, :].reshape(64, 256)], axis=1)
-        XF[...] = XF[...] + change
-        yield
-
-    def ring_reduce(src, ub, db, ts, tb, ybuf, result, block_done):
-        def part(off, h):
-            return src.at[pl.ds(mo(((z + off + 8) % 8) * 64 + h * 32, 32), 32), :]
-
-        us = {(k, h): wire.slot() for k in range(4) for h in range(2)}
-        ds = {(k, h): wire.slot() for k in range(4) for h in range(2)}
-        block_done(4)
-        wire.send(part(4, 0), ub.at[0, 0:32, :], us[0, 0], ups)
-        wire.send(part(4, 1), db.at[0, 32:64, :], ds[0, 1], downs)
-        for k in (1, 2, 3):
-            block_done(4 - k)
-            yield
-            for h in ((1, 0) if k == 1 else (0, 1)):
-                hu, hd = h, 1 - h
-                if k > 1 or hu == 0:
-                    got = ub.at[k - 1, hu * 32:hu * 32 + 32, :]
-                    wire.recv(got, us[k - 1, hu], downs)
-                    acc = part(4 - k, hu)
-                    acc[...] = (acc[...].astype(F32) + got[...].astype(F32)).astype(BF)
-                wire.send(part(4 - k, hu), ub.at[k, hu * 32:hu * 32 + 32, :], us[k, hu], ups)
-                if k > 1 or hd == 1:
-                    got = db.at[k - 1, hd * 32:hd * 32 + 32, :]
-                    wire.recv(got, ds[k - 1, hd], ups)
-                    acc = part(k - 4, hd)
-                    acc[...] = (acc[...].astype(F32) + got[...].astype(F32)).astype(BF)
-                wire.send(part(k - 4, hd), db.at[k, hd * 32:hd * 32 + 32, :], ds[k, hd], downs)
-        yield
-        for h in (0, 1):
-            a, b = ub.at[3, h * 32:h * 32 + 32, :], db.at[3, h * 32:h * 32 + 32, :]
-            wire.recv(a, us[3, h], downs)
-            wire.recv(b, ds[3, h], ups)
-            total = part(0, h)[...].astype(F32) + a[...].astype(F32) + b[...].astype(F32)
-            ts[h * 32:h * 32 + 32, :] = total
-            tb[h * 32:h * 32 + 32, :] = total.astype(BF)
+            wire.recv(blk16(za, -d), zg[d], zs[8 - d])
+        got = za[...].astype(F32).reshape(8, 16, 256)
+        result.append(jnp.concatenate(
+            [got[:, 0:8, :].reshape(64, 256), got[:, 8:16, :].reshape(64, 256)], axis=1))
+        yield
+
+    def z_reduce(result, blocks):
+        def part(off, lo=0, count=64):
+            return D.at[pl.ds(mo(((z + off + 8) % 8) * 64 + lo, 32), count), :]
+
+        s4 = [wire.slot() for _ in range(2)]
+        s3 = [wire.slot() for _ in range(2)]
+        s1 = [wire.slot() for _ in range(2)]
+        s2 = [wire.slot() for _ in range(2)]
+        blocks((4, 0))
+        wire.send(part(4, 0, 32), q4.at[0], s4[0], zs[2])
+        wire.send(part(4, 32, 32), q4.at[1], s4[1], zs[6])
+        blocks((3, 5))
+        wire.send(part(3), q3.at[0], s3[0], zs[1])
+        wire.send(part(5), q3.at[1], s3[1], zs[7])
+        blocks((2, 6))
+        blocks((1, 7))
+        wire.send(part(1), n1.at[0], s1[0], zs[1])
+        wire.send(part(7), n1.at[1], s1[1], zs[7])
+        yield
+        for n, (off, near, far) in enumerate(((2, 7, 6), (6, 1, 2))):
+            wire.recv(q3.at[n], s3[n], zs[near])
+            wire.recv(q4.at[n], s4[n], zs[far])
+            acc = part(off)
+            total = acc[...].astype(F32) + q3[n].astype(F32)
+            both = [total[0:32], total[32:64]]
+            both[n] = both[n] + q4[n].astype(F32)
+            acc[...] = jnp.concatenate(both, axis=0).astype(BF)
+            wire.send(acc, n2.at[n], s2[n], zs[off])
+        yield
+        total = part(0)[...].astype(F32)
+        for n in range(2):
+            wire.recv(n1.at[n], s1[n], zs[(7, 1)[n]])
+            wire.recv(n2.at[n], s2[n], zs[(6, 2)[n]])
+            total = total + n1[n].astype(F32) + n2[n].astype(F32)
+        tsum[...] = total
+        tbf[...] = total.astype(BF)
         ys = {j: wire.slot() for j in (1, 2, 3)}
         for j in (2, 1, 3):
-            wire.send(tb.at[pl.ds(mo(((yh + j) % 4) * 16, 16), 16), :], ybuf.at[j - 1], ys[j], yhs[j])
-        yield
-        total = ts[pl.ds(mo(yh * 16, 16), 16), :]
+            wire.send(tbf.at[pl.ds(mo(((yh + j) % 4) * 16, 16), 16), :], yb.at[j - 1], ys[j], yhs[j])
+        yield
+        total = tsum[pl.ds(mo(yh * 16, 16), 16), :]
         for j in (1, 3, 2):
-            wire.recv(ybuf.at[j - 1], ys[j], yhs[4 - j])
-            total = total + ybuf[j - 1].astype(F32)
+            wire.recv(yb.at[j - 1], ys[j], yhs[4 - j])
+            total = total + yb[j - 1].astype(F32)
         result.append(total)
         yield
 
     def bulk():
-        for b in range(4):
-            part_cols = []
-            for q in range(4):
-                lo = b * 128 + q * 32
-                v = X[lo:lo + 32, :].astype(F32)
-                XG[lo:lo + 32, :] = (v * g).astype(BF)
-                part_cols.append(jnp.sum(v * v, axis=1, keepdims=True))
-            col = jnp.concatenate(part_cols, axis=0)
-            SS[b:b + 1, :] = jnp.sum(jnp.where(eye(128, 128), col, 0.0), axis=0, keepdims=True)
-        SS[4:8, :] = jnp.zeros((4, 128), F32)
-
-        def gate_up(row0, p, dst):
-            @pl.loop(0, 2)
-            def _(i):
-                r = mo(i * 128, 128)
-                dst[pl.ds(r, 128), cols(p)] = jnp.dot(
-                    XG[pl.ds(mo(row0 + r, 128), 128), :], W[:, cols(p)],
-                    preferred_element_type=F32).astype(BF)
-
-        cslot = [wire.slot() for _ in range(NG)]
-        for p in range(NG):
-            gate_up((1 - c) * 256, p, snd)
-            wire.send(snd.at[:, cols(p)], crecv.at[:, cols(p)], cslot[p], core)
+        gate_up((3, 5))
+        gate_up((4,))
         sq = sq_rounds(SS, SSr)
         next(sq)
         yield
-        for p in range(NG):
-            gate_up(c * 256, p, own)
-        yield
 
         def blk(off, h):
             return pl.ds(mo(((x + off) % 4) * 64 + h * 32, 32), 32)
 
         xslot = [[wire.slot() for _ in range(6)] for _ in range(NG)]
-        for p in range(NG):
-            wire.recv(crecv.at[:, cols(p)], cslot[p], core)
-
+        for d in range(8):
+            wire.recv(crecv.at[unit_rows(d), :], cslot[d], core)
+        for p in range(NG):
             @pl.loop(0, 8)
             def _(i):
                 r = pl.ds(mo(i * 32, 32), 32)
-                own[r, cols(p)] = (own[r, cols(p)].astype(F32) + crecv[r, cols(p)].astype(F32)).astype(BF)
+                own[r, cols(p)] = (G[pl.ds(mo(i * 64 + c * 32, 32), 32), cols(p)].astype(F32)
+                                   + crecv[r, cols(p)].astype(F32)).astype(BF)
             wire.send(own.at[blk(2, 0), cols(p)], fwdp.at[:, cols(p)], xslot[p][0], xs[1])
             wire.send(own.at[blk(2, 1), cols(p)], fwdm.at[:, cols(p)], xslot[p][1], xs[3])
             wire.send(own.at[blk(1, 1), cols(p)], dirp.at[32:64, cols(p)], xslot[p][2], xs[1])
@@ -424,7 +434,7 @@
             wire.send(ysnd.at[:, cols(p)], yrecv.at[:, cols(p)], yslot[p], ydev)
             tot[:, cols(p)] = xsum(mine)
         yield
-        scale = scale_of(SSr, c * 256 + x * 64 + yl * 32, 32)
+        scale = scale_of(SSr, (x * 2 + yl) * 128 + c * 32, 32)
 
         def hrows(off, h):
             return pl.ds(mo(c * 256 + ((x + off) % 4) * 64 + h * 32, 32), 32)
@@ -475,18 +485,15 @@
         for p in range(NG):
             wire.recv(H.at[pl.ds(mo((1 - c) * 256, 256), 256), hcols(p)], hc[p], core)
 
-        def down_pair(off):
-            a = pl.ds(mo(((z + off) % 8) * 64, 64), 64)
-            b = pl.ds(mo(((z - off + 8) % 8) * 64, 64), 64)
-            if off == 4:
-                b = pl.ds(mo(z * 64, 64), 64)
-            both = jnp.concatenate([H[a, :], H[b, :]], axis=0)
+        def down_blocks(ds):
+            units = [pl.ds(mo(cc * 256 + ((z + d) % 8) * 32, 32), 32) for d in ds for cc in (0, 1)]
+            both = jnp.concatenate([H[u, :] for u in units], axis=0)
             prod = jnp.dot(both, WD[...], preferred_element_type=F32).astype(BF)
-            D[a, :] = prod[0:64]
-            D[b, :] = prod[64:128]
+            for n, d in enumerate(ds):
+                D[pl.ds(mo(((z + d) % 8) * 64, 64), 64), :] = prod[n * 64:n * 64 + 64]
 
         delta = []
-        for _ in ring_reduce(D, upb, dnb, tsum, tbf, yb, delta, down_pair):
+        for _ in z_reduce(delta, down_blocks):
             if not delta:
                 yield
         st[...] = tok_rows() + delta[0]
@@ -502,83 +509,62 @@
         for gen in gens:
             next(gen)
 
-    p1, big = packed(0), bulk()
+    p1, big = packed(0), (bulk() if upto not in (7, 70, 71, 72) else iter(int, 1))
+    if upto in (7, 70, 71, 72):
+        st[...] = tok_rows()
 
     def stop(*gens):
-        for gen in gens:
+        for gen in (gens if upto < 9 else ()):
             for _ in gen:
                 pass
-        load_down.wait()
         out[...] = XF[0:16, :].astype(BF)
         finish()
 
-    run(p1)
-    run(p1, big)
-    run(big)
-    run(p1)
-    run(p1)
-    run(p1)
-    load_down.wait()
-    if upto < 2:
+    SPEC = {2: 2, 5: 1, 6: 1, 7: 1, 8: 1, 10: 1, 11: 1, 12: 1, 15: 1, 16: 1, 17: 9}
+    count = [0]
+
+    def fast(gen):
+        next(gen)
+        count[0] += 1
+        if upto in (0, 7, 70, 71, 72):
+            return
+        for _ in range(SPEC.get(count[0], 0)):
+            if next(big, done) is done:
+                break
+
+    for _ in range(5):
+        fast(p1)
+        if count[0] == 4:
+            load_down.wait()
+    if upto == 70:
         return stop(big)
-    total = all_sum(down_of(0))
-    run(total)
-    run(big)
-    run(total)
-    run(big)
-    run(total)
-    run(big)
-    run(total)
-    if upto < 3:
+    change = []
+    total = all_sum(0, down_of(0), change)
+    for _ in range(4):
+        fast(total)
+    XF[...] = XF[...] + change[0]
+    if upto == 71:
         return stop(big)
     p2 = packed(1)
-    run(p2)
-    run(big)
-    run(p2)
-    run(big)
-    run(p2)
-    run(big)
-    run(p2)
-    run(big, p2)
-    run(big)
-
-    down2 = down_of(1).astype(BF)
+    for _ in range(5):
+        fast(p2)
+    if upto == 72:
+        return stop(big)
+
+    total = all_sum(1, down_of(1), change)
+    fast(total)
     counts = jnp.sum(flags, axis=1, keepdims=True)
-    before = jnp.sum(jnp.where(unit < owner, counts, 0.0), axis=0, keepdims=True)
-    here = jnp.sum(jnp.where(unit == owner, counts, 0.0), axis=0, keepdims=True)
-    slot_lane = lax.broadcasted_iota(jnp.int32, (1, 512), 1) % 16
-    place = (slot_lane % 8).astype(F32)
-    goal = jnp.where(place < here, before + place, -1.0)
-    hit = jnp.where(goal == want, 1.0, 0.0)
-    left = jnp.where(slot_lane < 8, hit, 0.0).astype(BF)
-    right = jnp.where(slot_lane >= 8, hit, 0.0).astype(BF)
-    dims = (((0,), (0,)), ((), ()))
-    D2[...] = (lax.dot_general(left, down2[:, 0:256], dims, preferred_element_type=F32)
-               + lax.dot_general(right, down2[:, 256:512], dims, preferred_element_type=F32)).astype(BF)
-    back = []
-    last = ring_reduce(D2, upb2, dnb2, tsum2, tbf2, yb2, back, lambda off: None)
-
-    for k in range(6):
-        run(last)
-        if k < 5:
-            for _ in range(1 if k else 2):
-                if next(big, done) is done:
-                    break
-    for _ in big:
-        pass
-    back = back[0]
+    before = jnp.sum(jnp.where(lax.broadcasted_iota(jnp.int32, (32, 1), 0) < t, counts, 0.0), axis=0, keepdims=True)
     act_row = (RV[...] == 2).astype(F32)
     sub = lax.broadcasted_iota(jnp.int32, (16, 16), 0)
     lane = lax.broadcasted_iota(jnp.int32, (16, 16), 1)
     act_col = jnp.sum(jnp.where(sub == lane, act_row, 0.0), axis=1, keepdims=True)
     place_col = jnp.sum(jnp.where(lane <= sub, act_row, 0.0), axis=1, keepdims=True) - 1.0
-    acc_l = jnp.zeros((16, 256), F32)
-    acc_r = jnp.zeros((16, 256), F32)
-    for k in range(8):
-        put = jnp.where((place_col == k) & (act_col > 0.5), 1.0, 0.0)
-        acc_l = acc_l + put * back[k:k + 1, :]
-        acc_r = acc_r + put * back[k + 8:k + 9, :]
-    out[...] = (st[...] + jnp.concatenate([acc_l, acc_r], axis=1)).astype(BF)
+    place = jnp.where(act_col > 0.5, before + place_col, -1.0)
+    take_rows = jnp.where(place == lax.broadcasted_iota(jnp.int32, (16, 64), 1).astype(F32), 1.0, 0.0).astype(BF)
+    for _ in range(3):
+        fast(total)
+    out[...] = (st[...] + jnp.dot(take_rows, change[1].astype(BF), preferred_element_type=F32)).astype(BF)
     finish()
 
 
@@ -587,15 +573,14 @@
     vf = lambda *shape: pltpu.VMEM(shape, F32)
     vspec, hbm = pl.BlockSpec(memory_space=pltpu.VMEM), pl.BlockSpec(memory_space=pltpu.MemorySpace.HBM)
     scratch = [
-        vm(512, 512), vm(512, 512), vm(512, 1792), vm(896, 512), vf(32, 1, 128), vf(1, 512),
-        pltpu.VMEM((1, 16), jnp.int32),
-        vm(256, 1792), vm(256, 1792), vm(256, 1792), vm(32, 1792), vm(32, 1792), vm(64, 1792), vm(64, 1792),
+        vm(512, 512), vm(512, 1792), vm(896, 512), vf(32, 1, 128), vf(1, 512), pltpu.VMEM((1, 16), jnp.int32),
+        vm(512, 1792), vm(256, 1792), vm(256, 1792), vm(32, 1792), vm(32, 1792), vm(64, 1792), vm(64, 1792),
         vm(32, 1792), vm(32, 1792), vf(32, 1792), vm(512, 896),
-        vm(512, 512), vm(4, 64, 512), vm(4, 64, 512), vf(64, 512), vm(64, 512), vm(3, 16, 512),
+        vm(512, 512), vm(2, 32, 512), vm(2, 64, 512), vm(2, 64, 512), vm(2, 64, 512),
+        vf(64, 512), vm(64, 512), vm(3, 16, 512),
         vf(8, 128), vf(10, 8, 128), vf(2, 8, 128), vf(2, 10, 8, 128), vm(512, 512), vm(128, 512),
         vf(64, 512), vm(2, 64, 512), vm(2, 64, 2048), vm(2, 32, 2048), vm(2, 7, 16, 512), vm(2, 64, 1024),
-        vm(128, 256), vm(7, 16, 256), vm(3, 16, 256), vm(16, 256), vm(128, 256),
-        vm(512, 256), vm(4, 64, 256), vm(4, 64, 256), vf(64, 256), vm(64, 256), vm(3, 16, 256),
+        vm(2, 128, 256), vm(2, 7, 16, 256), vm(2, 3, 16, 256), vm(2, 16, 256), vm(2, 128, 256),
         vf(16, 512),
         pltpu.SemaphoreType.DMA((12,)), pltpu.SemaphoreType.DMA((320,)), pltpu.SemaphoreType.DMA((320,)),
     ]
@@ -606,7 +591,7 @@
         out_specs=vspec,
         scratch_shapes=scratch,
         compiler_params=pltpu.CompilerParams(
-            collective_id=0, has_side_effects=True, vmem_limit_bytes=40 * 1024 * 1024),
+            collective_id=0, has_side_effects=True, vmem_limit_bytes=60 * 1024 * 1024),
         cost_estimate=pl.CostEstimate(flops=2000000000, bytes_accessed=3000000, transcendentals=30000),
         name="two_pass_block",
     )(tokens, norm_gain.reshape(1, 512), revisit.reshape(1, 16), gate_weight, up_weight, down_weight)

time: 101 us -> 88.8 us (0.88); the launches traced: 99.3 us -> 88.5 us
  Pallas kernels: 93.7 us -> 87.2 us
  local copies, waits for them, and re-layouts: 5.54 us -> 1.32 us
    pallas_call x1, Pallas kernels: 93.7 us -> 87.2 us  [body(): pl.pallas_call(functools.partial(kernel, upto), out_shape=jax.ShapeDtypeS...]
    unnamed x13 -> x1, local copies, waits for them, and re-layouts: 5.54 us -> 1.32 us
where the time goes in v3:
time: 88.8 us; the launch traced here: 88.5 us
  Pallas kernels  87.2 us (98%)
  local copies, waits for them, and re-layouts  1.32 us (1%)
    pallas_call x1, Pallas kernels, body(): pl.pallas_call(functools.partial(kernel, upto), out_shape=jax.ShapeDtypeS...  87.2 us

profile of v3, /device:TPU:1, one launch (start us, length us, event | category | flops | bytes accessed | tf_op | source)
XLA Modules:
  0.0 88.5 jit_solution(3572175049192916783)
XLA Ops:
  0.0 87.2 %two_pass_block.1 = bf16[16,512]{1,0:T(8,128)(2,1)} custom-call(bf16[16,512]{1,0:T(8,128)(2,1)} %tok.1, f32[1,512]{1,0:T(1,128)} %bitcast.2, s32[1,16]{1,0:T(1,128)} %bitcast.3, bf16[512,896]{1,0:T(8,128)(2,1)} %wg.1, bf16[512,896]{1,0:T(8,128)(2,1)} %wu.1, bf16[896,512]{1,0:T(8,128)(2,1)} %wd.1), custom_call_target="tpu_custom_call" | custom-call | flops 2000000000 | bytes 3000000 | tf_op jit(solution)/shard_map/two_pass_block/pallas_call | solution.py:587
  87.2 1.3 %copy.8 = bf16[16,512]{1,0:T(8,128)(2,1)} copy(bf16[16,512]{1,0:T(8,128)(2,1)} %two_pass_block.1) | data formatting | bytes 32768

commit v4 on v3

--- a/solution.py
+++ b/solution.py
@@ -52,7 +52,7 @@
 def kernel(upto, tok, gain, rev, wg, wu, wd, out,
            X, W, WD, F, GN, RV, G, own, crecv, fwdp, fwdm, dirp, dirm, ysnd, yrecv, tot, H,
            D, q4, q3, n1, n2, tsum, tbf, yb, SS, SSr, S2, S2r, TRI, SPR,
-           XF, C, G2, c2r, x2r, H2, PF, zr, z3, yex, ZA, st,
+           CH, XF, C, G2, c2r, x2r, H2, PF, zr, z3, yex, ZA, st,
            wsem, send_sem, recv_sem):
     s, t = lax.axis_index("section"), lax.axis_index("tp")
     c, x, yl = s % 2, (s // 2) % 4, s // 8
@@ -121,10 +121,14 @@
         same(rows(0, 0), sy[j], yhs[j])
 
     def spread(j):
-        for d in (2, 6, 1, 7):
+        for d in ((2, 6, 1, 7) if 'drrr'[j] == 'r' else (4, 3, 5, 2, 6, 1, 7)):
             same(rows(0, j), sz[d, j], zs[d])
 
     def relay(j):
+        if 'drrr'[j] == 'd':
+            wire.recv(rows(-2, j), sz[2, j], zs[6])
+            wire.recv(rows(2, j), sz[6, j], zs[2])
+            return
         wire.recv(rows(-2, j), sz[2, j], zs[6])
         if j in (0, 1):
             same(rows(-2, j), sz[4, j], zs[2])
@@ -171,6 +175,11 @@
                 G[b, cols(p)] = prod[n * 64:n * 64 + 64]
         for d in ds:
             wire.send(G.at[half_rows(d, 1 - c), :], crecv.at[unit_rows(d), :], cslot[d], core)
+
+    def pair_sum(d):
+        r = unit_rows(d)
+        wire.recv(crecv.at[r, :], cslot[d], core)
+        own[r, :] = (G[half_rows(d, c), :].astype(F32) + crecv[r, :].astype(F32)).astype(BF)
 
     spread(0)
     for j in (1, 3):
@@ -198,19 +207,15 @@
     take(1)
     if upto not in (0, 7, 70, 71, 72):
         gate_up((1, 7))
+        pair_sum(0)
         gate_up((2, 6))
+        pair_sum(1)
+        pair_sum(7)
     wire.recv(frow(-1), fz[1], zs[7])
     wire.recv(frow(1), fz[7], zs[1])
     wire.recv(frow(-3), fz[3], zs[7])
     wire.recv(frow(3), fz[5], zs[1])
     wire.recv(frow(4), fz[4], zs[6])
-    take(3)
-    take(4)
-    if upto < 1:
-        load_down.wait()
-        out[...] = X[my_rows, :]
-        return finish()
-
     flags = F[...].reshape(32, 128)
     lanes = jnp.dot(flags.astype(BF), SPR[...], preferred_element_type=F32)
     owner = lax.broadcasted_iota(jnp.int32, (32, 512), 1) // 16
@@ -220,7 +225,15 @@
     want = lax.broadcasted_iota(jnp.int32, (64, 512), 0).astype(F32)
     goal = jnp.where(active > 0.5, upto_here - 1.0, -1.0)
     choose = jnp.where(goal == want, 1.0, 0.0).astype(BF)
-    XF[...] = jnp.dot(choose, X[...], preferred_element_type=F32)
+    CH[...] = choose
+    take(3)
+    take(4)
+    if upto < 1:
+        load_down.wait()
+        out[...] = X[my_rows, :]
+        return finish()
+
+    XF[...] = jnp.dot(CH[...], X[...], preferred_element_type=F32)
 
     def sq_rounds(ss, rr):
         slots = [wire.slot() for _ in range(8)]
@@ -254,6 +267,9 @@
         s2[...] = jnp.zeros((8, 128), F32)
         s2[0:1, :] = jnp.sum(jnp.where(eye(64, 128), col, 0.0), axis=0, keepdims=True)
         g2, h2all = G2.at[n], H2.at[n]
+        away = pl.ds(mo((1 - c) * 32, 32), 32)
+        core_rows = pl.ds(mo(c * 32, 32), 32)
+        group = [wire.slot() for _ in range(NG)]
         for p in range(NG):
             lo, w = GROUPS[p]
             prod = jnp.dot(C[n], W[:, cols(p)], preferred_element_type=F32).astype(BF)
@@ -262,14 +278,14 @@
             if w < 256:
                 g2[:, 512 * p + w:512 * p + 256] = jnp.zeros((64, 256 - w), BF)
                 g2[:, 512 * p + 256 + w:512 * p + 512] = jnp.zeros((64, 256 - w), BF)
-        slot = wire.slot()
-        wire.send(g2.at[pl.ds(mo((1 - c) * 32, 32), 32), :], c2r.at[n], slot, core)
+            wire.send(g2.at[away, 512 * p:512 * p + 512], c2r.at[n, :, 512 * p:512 * p + 512], group[p], core)
         sq = sq_rounds(s2, S2r.at[n])
         next(sq)
         yield
-        core_rows = pl.ds(mo(c * 32, 32), 32)
-        wire.recv(c2r.at[n], slot, core)
-        g2[core_rows, :] = (g2[core_rows, :].astype(F32) + c2r[n].astype(F32)).astype(BF)
+        for p in range(NG):
+            wide = slice(512 * p, 512 * p + 512)
+            wire.recv(c2r.at[n, :, wide], group[p], core)
+            g2[core_rows, wide] = (g2[core_rows, wide].astype(F32) + c2r[n, :, wide].astype(F32)).astype(BF)
 
         def block(dx, dy):
             return g2.at[pl.ds(mo(c * 32 + ((yl + dy) % 2) * 16, 16), 16), pl.ds(mo(((x + dx) % 4) * 512, 512), 512)]
@@ -394,14 +410,9 @@
             return pl.ds(mo(((x + off) % 4) * 64 + h * 32, 32), 32)
 
         xslot = [[wire.slot() for _ in range(6)] for _ in range(NG)]
-        for d in range(8):
-            wire.recv(crecv.at[unit_rows(d), :], cslot[d], core)
-        for p in range(NG):
-            @pl.loop(0, 8)
-            def _(i):
-                r = pl.ds(mo(i * 32, 32), 32)
-                own[r, cols(p)] = (G[pl.ds(mo(i * 64 + c * 32, 32), 32), cols(p)].astype(F32)
-                                   + crecv[r, cols(p)].astype(F32)).astype(BF)
+        for d in (2, 6, 3, 5, 4):
+            pair_sum(d)
+        for p in range(NG):
             wire.send(own.at[blk(2, 0), cols(p)], fwdp.at[:, cols(p)], xslot[p][0], xs[1])
             wire.send(own.at[blk(2, 1), cols(p)], fwdm.at[:, cols(p)], xslot[p][1], xs[3])
             wire.send(own.at[blk(1, 1), cols(p)], dirp.at[32:64, cols(p)], xslot[p][2], xs[1])
@@ -520,7 +531,7 @@
         out[...] = XF[0:16, :].astype(BF)
         finish()
 
-    SPEC = {2: 2, 5: 1, 6: 1, 7: 1, 8: 1, 10: 1, 11: 1, 12: 1, 15: 1, 16: 1, 17: 9}
+    SPEC = {2: 2, 4: 1, 6: 1, 7: 1, 8: 1, 9: 1, 11: 1, 12: 1, 15: 1, 16: 1, 17: 9}
     count = [0]
 
     def fast(gen):
@@ -579,7 +590,7 @@
         vm(512, 512), vm(2, 32, 512), vm(2, 64, 512), vm(2, 64, 512), vm(2, 64, 512),
         vf(64, 512), vm(64, 512), vm(3, 16, 512),
         vf(8, 128), vf(10, 8, 128), vf(2, 8, 128), vf(2, 10, 8, 128), vm(512, 512), vm(128, 512),
-        vf(64, 512), vm(2, 64, 512), vm(2, 64, 2048), vm(2, 32, 2048), vm(2, 7, 16, 512), vm(2, 64, 1024),
+        vm(64, 512), vf(64, 512), vm(2, 64, 512), vm(2, 64, 2048), vm(2, 32, 2048), vm(2, 7, 16, 512), vm(2, 64, 1024),
         vm(2, 128, 256), vm(2, 7, 16, 256), vm(2, 3, 16, 256), vm(2, 16, 256), vm(2, 128, 256),
         vf(16, 512),
         pltpu.SemaphoreType.DMA((12,)), pltpu.SemaphoreType.DMA((320,)), pltpu.SemaphoreType.DMA((320,)),

time: 88.8 us -> 87.5 us (0.985)
  Pallas kernels: 87.2 us -> 85.8 us
    pallas_call x1, Pallas kernels: 87.2 us -> 85.8 us  [body(): pl.pallas_call(functools.partial(kernel, upto), out_shape=jax.ShapeDtypeS...]
where the time goes in v4:
time: 87.5 us; the launch traced here: 87.2 us
  Pallas kernels  85.8 us (98%)
  local copies, waits for them, and re-layouts  1.32 us (2%)
    pallas_call x1, Pallas kernels, body(): pl.pallas_call(functools.partial(kernel, upto), out_shape=jax.ShapeDtypeS...  85.8 us

profile of v4, /device:TPU:1, one launch (start us, length us, event | category | flops | bytes accessed | tf_op | source)
XLA Modules:
  0.0 87.2 jit_solution(9099512874740612656)
XLA Ops:
  0.0 85.8 %two_pass_block.1 = bf16[16,512]{1,0:T(8,128)(2,1)} custom-call(bf16[16,512]{1,0:T(8,128)(2,1)} %tok.1, f32[1,512]{1,0:T(1,128)} %bitcast.2, s32[1,16]{1,0:T(1,128)} %bitcast.3, bf16[512,896]{1,0:T(8,128)(2,1)} %wg.1, bf16[512,896]{1,0:T(8,128)(2,1)} %wu.1, bf16[896,512]{1,0:T(8,128)(2,1)} %wd.1), custom_call_target="tpu_custom_call" | custom-call | flops 2000000000 | bytes 3000000 | tf_op jit(solution)/shard_map/two_pass_block/pallas_call | solution.py:598
  85.9 1.3 %copy.8 = bf16[16,512]{1,0:T(8,128)(2,1)} copy(bf16[16,512]{1,0:T(8,128)(2,1)} %two_pass_block.1) | data formatting | bytes 32768
